TPU v7x, 32 devices: a whole 2x2x4 slice. The times are simulated.
32 devices in a mesh: seq: 4 (over y, x), fsdp: 8 (over z, core).
Axes of the slice: x: 2, y: 2, z: 4, core: 2. Of those that a mesh axis runs over, the one named last changes fastest.
Arguments:
- hidden_in: bfloat16 [8, 2048, 768], P('fsdp', 'seq'), may hold values from -6 to 6
- norm_gain: float32 [768], replicated, may hold values from 0.5 to 1.5
- w_in: bfloat16 [768, 3352], P('fsdp'), may hold values from -0.21875 to 0.21875
- conv_weight: float32 [4, 1792], replicated, may hold values from -3 to 3
- conv_bias: float32 [1792], replicated, may hold values from -1.5 to 1.5
- dt_bias: float32 [24], replicated, may hold values from -4 to -1
- a_log: float32 [24], replicated, may hold values from -4 to 2.8
- skip_gain: float32 [24], replicated, may hold values from 0.1 to 1
- gate_gain: float32 [1536], replicated, may hold values from 0.5 to 1.5
- w_out: bfloat16 [1536, 768], P('fsdp'), may hold values from -0.15625 to 0.15625
- cotangent: bfloat16 [8, 2048, 768], P('fsdp', 'seq'), may hold values from -6 to 6
Outputs:
- layer_out: bfloat16 [8, 2048, 768], P('fsdp', 'seq')
- d_hidden: float32 [8, 2048, 768], P('fsdp', 'seq')
- d_norm_gain: float32 [768], replicated
- d_w_in: float32 [768, 3352], P('fsdp')
- d_conv_weight: float32 [4, 1792], replicated
- d_conv_bias: float32 [1792], replicated
- d_dt_bias: float32 [24], replicated
- d_a_log: float32 [24], replicated
- d_skip_gain: float32 [24], replicated
- d_gate_gain: float32 [1536], replicated
- d_w_out: float32 [1536, 768], P('fsdp')
All inputs are finite; a program needn't handle non-finite values.
Results may differ from a plain program's by a relative error of at most 0.012.
Values may be sent and summed in bfloat16 or wider, within the bound.
A program may use at most 128 MiB of HBM per device.

v0:
```python
import jax
import jax.numpy as jnp
from jax import lax
from jax.sharding import PartitionSpec as P

D = 768
HEADS = 24
HEAD_DIM = 64
STATE = 128
CONVW = 4
SPAN = 256
INNER = 1536


epsilon = 1e-05
precise = lax.Precision.HIGHEST


def causal_conv(values, kernel):
    length = values.shape[0]
    padded = jnp.pad(values, ((CONVW - 1, 0), (0, 0)))
    summed = kernel[0] * padded[0:length]
    for offset in range(1, CONVW):
        summed = summed + kernel[offset] * padded[offset : offset + length]
    return summed


def state_scan(values, b_rows, c_rows, step_size, decay_rates):
    length, head_count, head_dim = values.shape
    block_count = length // SPAN
    causal_mask = jnp.arange(SPAN)[:, None] >= jnp.arange(SPAN)[None, :]

    def block_step(carried, pieces):
        x_block, b_block, c_block, dt_block = pieces
        decay_sum = jnp.cumsum(dt_block * decay_rates[None, :], axis=0)
        decay_cols = decay_sum.T
        intersection = jnp.dot(c_block, b_block.T, precision=precise)
        spread = jnp.where(causal_mask[None], decay_cols[:, :, None] - decay_cols[:, None, :], 0.0)
        factor = jnp.where(causal_mask[None], jnp.exp(spread), 0.0)
        mixing = factor * intersection[None] * dt_block.T[:, None, :]
        within = jnp.einsum("hts,shp->thp", mixing, x_block, precision=precise)
        earlier = (
            jnp.einsum("tn,hpn->thp", c_block, carried, precision=precise)
            * jnp.exp(decay_sum)[:, :, None]
        )
        remain = jnp.exp(decay_sum[-1][None, :] - decay_sum) * dt_block
        renewed = carried * jnp.exp(decay_sum[-1])[:, None, None] + jnp.einsum(
            "sh,shp,sn->hpn", remain, x_block, b_block, precision=precise
        )
        return (renewed, within + earlier)

    initial = jnp.zeros((head_count, head_dim, b_rows.shape[1]), values.dtype)
    blocks = (
        values.reshape(block_count, SPAN, head_count, head_dim),
        b_rows.reshape(block_count, SPAN, b_rows.shape[1]),
        c_rows.reshape(block_count, SPAN, c_rows.shape[1]),
        step_size.reshape(block_count, SPAN, head_count),
    )
    final_state, outputs = lax.scan(jax.checkpoint(block_step), initial, blocks)
    return outputs.reshape(length, head_count, head_dim)


def mixer_local(x_in, bc_in, dt_in, conv_x, conv_bc, bias_x, bias_bc, dt_shift, a_decay, skip_vals):
    length = x_in.shape[0]
    head_count = dt_in.shape[1]
    x_conv = jax.nn.silu(causal_conv(x_in, conv_x) + bias_x)
    bc_conv = jax.nn.silu(causal_conv(bc_in, conv_bc) + bias_bc)
    step_size = jax.nn.softplus(dt_in + dt_shift)
    decay_rates = -jnp.exp(a_decay)
    values = x_conv.reshape(length, head_count, HEAD_DIM)
    scanned = state_scan(values, bc_conv[:, :STATE], bc_conv[:, STATE:], step_size, decay_rates)
    return (scanned + skip_vals[None, :, None] * values).reshape(length, head_count * HEAD_DIM)


def times_transposed(left_mat, right_mat):
    return lax.dot_general(
        left_mat, right_mat, (((1,), (1,)), ((), ())), preferred_element_type=jnp.float32
    )


def over_rows(left_mat, right_mat):
    return lax.dot_general(
        left_mat, right_mat, (((0,), (0,)), ((), ())), preferred_element_type=jnp.float32
    )


def fsdp_rows(first, second):
    return (
        lax.psum_scatter(first, "fsdp", scatter_dimension=0, tiled=True),
        lax.psum_scatter(second, "fsdp", scatter_dimension=0, tiled=True),
    )


def seq_total(first, second):
    return lax.psum((first, second), "seq")


def body(
    hidden_in,
    norm_gain,
    w_in,
    conv_weight,
    conv_bias,
    dt_bias,
    a_log,
    skip_gain,
    gate_gain,
    w_out,
    cotangent,
):
    w_in_full, w_out_full = (
        lax.all_gather(w_in, "fsdp", axis=0, tiled=True),
        lax.all_gather(w_out, "fsdp", axis=0, tiled=True),
    )
    seq_count = lax.axis_size("seq")
    seq_rank = lax.axis_index("seq")
    head_local = HEADS // seq_count
    chan_local = head_local * HEAD_DIM
    chan_start = seq_rank * chan_local
    head_start = seq_rank * head_local
    tokens = hidden_in[0].astype(jnp.float32)
    inv_rms = lax.rsqrt(jnp.mean(tokens * tokens, axis=1, keepdims=True) + epsilon)
    normed_in = (tokens * inv_rms * norm_gain).astype(jnp.bfloat16)
    projected = jnp.dot(normed_in, w_in_full, preferred_element_type=jnp.float32).astype(
        jnp.bfloat16
    )
    gate_vals = projected[:, :INNER]
    x_vals = projected[:, INNER : 2 * INNER]
    bc_vals = projected[:, 2 * INNER : 2 * INNER + 2 * STATE]
    dt_vals = projected[:, 2 * INNER + 2 * STATE :]
    x_whole, dt_whole, gate_whole = (
        lax.all_to_all(x_vals, "seq", split_axis=1, concat_axis=0, tiled=True),
        lax.all_to_all(dt_vals, "seq", split_axis=1, concat_axis=0, tiled=True),
        lax.all_to_all(gate_vals, "seq", split_axis=1, concat_axis=0, tiled=True),
    )
    bc_whole = lax.all_gather(bc_vals, "seq", axis=0, tiled=True)
    conv_x = lax.dynamic_slice_in_dim(conv_weight, chan_start, chan_local, 1)
    conv_bc = conv_weight[:, INNER:]
    bias_x = lax.dynamic_slice_in_dim(conv_bias, chan_start, chan_local, 0)
    bias_bc = conv_bias[INNER:]
    shift_local = lax.dynamic_slice_in_dim(dt_bias, head_start, head_local, 0)
    decay_local = lax.dynamic_slice_in_dim(a_log, head_start, head_local, 0)
    skip_local = lax.dynamic_slice_in_dim(skip_gain, head_start, head_local, 0)
    gain_local = lax.dynamic_slice_in_dim(gate_gain, chan_start, chan_local, 0)
    mixed_raw, mixer_back = jax.vjp(
        mixer_local,
        x_whole.astype(jnp.float32),
        bc_whole.astype(jnp.float32),
        dt_whole.astype(jnp.float32),
        conv_x,
        conv_bc,
        bias_x,
        bias_bc,
        shift_local,
        decay_local,
        skip_local,
    )
    mixed_f = lax.optimization_barrier(mixed_raw.astype(jnp.bfloat16)).astype(jnp.float32)
    gate_f = gate_whole.astype(jnp.float32)
    gate_silu = jax.nn.silu(gate_f)
    gated_vals = mixed_f * gate_silu
    square_sum = lax.psum(jnp.sum(gated_vals * gated_vals, axis=1), "seq")
    gate_rms = lax.rsqrt(square_sum / INNER + epsilon)[:, None]
    normed_head = (gated_vals * gate_rms * gain_local).astype(jnp.bfloat16)
    normed_out = lax.all_to_all(normed_head, "seq", split_axis=0, concat_axis=1, tiled=True)
    branch_out = jnp.dot(normed_out, w_out_full, preferred_element_type=jnp.float32)
    result = (tokens + branch_out).astype(jnp.bfloat16)
    grad_out = cotangent[0]
    d_normed = times_transposed(grad_out, w_out_full).astype(jnp.bfloat16)
    d_w_out_part = over_rows(normed_out, grad_out)
    d_head = lax.all_to_all(d_normed, "seq", split_axis=1, concat_axis=0, tiled=True).astype(
        jnp.float32
    )
    d_gain_local = jnp.sum(d_head * gated_vals * gate_rms, axis=0)
    cross_sum = lax.psum(jnp.sum(d_head * gain_local * gated_vals, axis=1), "seq")
    d_gated = (
        gate_rms * gain_local * d_head - gated_vals * gate_rms**3 * (cross_sum / INNER)[:, None]
    )
    gate_sigmoid = jax.nn.sigmoid(gate_f)
    d_mixed = lax.optimization_barrier((d_gated * gate_silu).astype(jnp.bfloat16)).astype(
        jnp.float32
    )
    d_gate = (d_gated * mixed_f * gate_sigmoid * (1.0 + gate_f * (1.0 - gate_sigmoid))).astype(
        jnp.bfloat16
    )
    d_x, d_bc, d_dt, d_conv_x, d_conv_bc, d_bias_x, d_bias_bc, d_shift, d_decay, d_skip = (
        mixer_back(d_mixed)
    )
    d_bc_seq = lax.psum_scatter(d_bc, "seq", scatter_dimension=0, tiled=True).astype(jnp.bfloat16)
    d_x_seq, d_dt_seq, d_gate_seq = (
        lax.all_to_all(d_x.astype(jnp.bfloat16), "seq", split_axis=0, concat_axis=1, tiled=True),
        lax.all_to_all(d_dt.astype(jnp.bfloat16), "seq", split_axis=0, concat_axis=1, tiled=True),
        lax.all_to_all(d_gate, "seq", split_axis=0, concat_axis=1, tiled=True),
    )
    d_proj = jnp.concatenate([d_gate_seq, d_x_seq, d_bc_seq, d_dt_seq], axis=1)
    d_normed_in = times_transposed(d_proj, w_in_full)
    d_w_in_part = over_rows(normed_in, d_proj)
    rows_in, rows_out = fsdp_rows(d_w_in_part, d_w_out_part)
    grad_w_in, grad_w_out = seq_total(rows_in, rows_out)
    d_norm_gain = jnp.sum(d_normed_in * tokens * inv_rms, axis=0)
    norm_cross = jnp.sum(d_normed_in * norm_gain * tokens, axis=1, keepdims=True)
    d_tokens = (
        inv_rms * norm_gain * d_normed_in
        - tokens * inv_rms**3 * norm_cross / D
        + grad_out.astype(jnp.float32)
    )
    conv_grad = jnp.concatenate(
        [
            lax.dynamic_update_slice_in_dim(
                jnp.zeros((CONVW, INNER), jnp.float32), d_conv_x, chan_start, 1
            ),
            d_conv_bc,
        ],
        axis=1,
    )
    bias_grad = jnp.concatenate(
        [
            lax.dynamic_update_slice_in_dim(
                jnp.zeros((INNER,), jnp.float32), d_bias_x, chan_start, 0
            ),
            d_bias_bc,
        ],
        axis=0,
    )
    shift_grad = lax.dynamic_update_slice_in_dim(
        jnp.zeros((HEADS,), jnp.float32), d_shift, head_start, 0
    )
    decay_grad = lax.dynamic_update_slice_in_dim(
        jnp.zeros((HEADS,), jnp.float32), d_decay, head_start, 0
    )
    skip_grad = lax.dynamic_update_slice_in_dim(
        jnp.zeros((HEADS,), jnp.float32), d_skip, head_start, 0
    )
    gain_grad = lax.dynamic_update_slice_in_dim(
        jnp.zeros((INNER,), jnp.float32), d_gain_local, chan_start, 0
    )
    small_sums = lax.psum(
        (d_norm_gain, conv_grad, bias_grad, shift_grad, decay_grad, skip_grad, gain_grad),
        ("seq", "fsdp"),
    )
    return (
        result[None],
        d_tokens[None],
        small_sums[0],
        grad_w_in,
        small_sums[1],
        small_sums[2],
        small_sums[3],
        small_sums[4],
        small_sums[5],
        small_sums[6],
        grad_w_out,
    )


def solution(mesh):
    placed = (
        P("fsdp", "seq", None),
        P(),
        P("fsdp", None),
        P(),
        P(),
        P(),
        P(),
        P(),
        P(),
        P("fsdp", None),
        P("fsdp", "seq", None),
    )
    return jax.shard_map(
        body,
        mesh=mesh,
        in_specs=placed,
        out_specs=(
            P("fsdp", "seq", None),
            P("fsdp", "seq", None),
            P(),
            P("fsdp", None),
            P(),
            P(),
            P(),
            P(),
            P(),
            P(),
            P("fsdp", None),
        ),
        check_vma=False,
    )
```

profile of v0, /device:TPU:0, one launch (start us, length us, event | category | flops | bytes accessed | tf_op | source)
XLA Modules:
  0.0 1019.6 jit_solution(17187587308190026661)
XLA Ops:
  11.9 57.1 %all-gather.4.cloned.1.call-done = bf16[768,3352]{1,0:T(8,128)(2,1)} async-done(((bf16[96,3352]{1,0:T(8,128)(2,1)}), bf16[768,3352]{1,0:T(8,128)(2,1)}) %all-gather.4.cloned.1.call-update) | async-done | bytes 5148688 | tf_op jit(solution)/shard_map/all_gather | solution.py:112
  126.7 11.4 %all-gather.6.cloned.1.call-done = bf16[2048,256]{0,1:T(8,128)(2,1)} async-done(((bf16[512,256]{0,1:T(8,128)(2,1)}), bf16[2048,256]{0,1:T(8,128)(2,1)}) %all-gather.6.cloned.1.call-update) | async-done | bytes 1048592 | tf_op jit(solution)/shard_map/all_gather | solution.py:136
  151.2 199.0 %while.44 = (s32[]{:T(128)}, f32[6,64,128]{2,1,0:T(8,128)S(1)}, f32[8,256,6,64]{1,0,3,2:T(8,128)}, f32[8,6,64,128]{3,2,1,0:T(8,128)}, f32[8,256,6]{1,2,0:T(8,128...) while((s32[]{:T(128)}, f32[6,64,128]{2,1,0:T(8,128)S(1)}, ...), condition=%wide.region_4.5_spmd.clone.clone, body=%wide.region_1.4_spmd.clone.clone.sunk | while | flops 707351040 | bytes 5774856 | solution.py:59
  166.2 9.8 dynamic_update_slice.101
  191.1 9.8 dynamic_update_slice.101
  216.0 9.8 dynamic_update_slice.101
  240.8 9.8 dynamic_update_slice.101
  265.7 9.8 dynamic_update_slice.101
  290.6 9.8 dynamic_update_slice.101
  369.7 17.0 %psum.77 = f32[2048]{0:T(1024)S(1)} all-reduce(f32[2048]{0:T(1024)S(1)} %multiply_reduce_fusion.9), channel_id=1, replica_groups=mesh['seq'=4,'fsdp'=8] {'seq'}, use_global_device_ids=true, to_apply=%region_6.7 | all-reduce | flops 2048 | bytes 16384 | tf_op jit(solution)/shard_map/psum | solution.py:162
  416.3 293.8 %while.43 = (s32[]{:T(128)}, f32[6]{0:T(128)S(1)}, f32[6,64,128]{2,1,0:T(8,128)S(1)}, f32[8,256,6,64]{1,0,3,2:T(8,128)}, f32[8,256,128]{2,1,0:T(8,128)}, /*index...) while((s32[]{:T(128)}, f32[6]{0:T(128)S(1)}, ...), condition=%wide.region_22.23_spmd.clone, body=%wide.region_9.22_spmd.clone.sunk | while | flops 1670427136 | bytes 14930680 | solution.py:59
  443.4 9.9 dynamic_update_slice.99
  480.1 9.9 dynamic_update_slice.99
  516.8 9.9 dynamic_update_slice.99
  553.5 9.9 dynamic_update_slice.99
  590.2 9.9 dynamic_update_slice.99
  626.9 9.9 dynamic_update_slice.99
  663.6 9.9 dynamic_update_slice.99
  700.3 9.9 dynamic_update_slice.99
  726.4 30.8 %all_to_all.125 = bf16[4,512,384]{1,2,0:T(8,128)(2,1)S(1)} all-to-all(bf16[4,512,384]{1,2,0:T(8,128)(2,1)S(1)} %copy.312), channel_id=1, replica_groups=mesh['seq'=4,'fsdp'=8] {'seq'}, dimensions={0} | all-to-all | bytes 3145728 | tf_op jit(solution)/shard_map/all_to_all | solution.py:165
  801.3 17.5 %all-to-all-done.6 = bf16[4,512,384]{1,2,0:T(8,128)(2,1)S(1)} async-done(((bf16[4,512,384]{1,2,0:T(8,128)(2,1)}), bf16[4,512,384]{1,2,0:T(8,128)(2,1)S(1)}, u32[]{:S(2)}, u32[]{:S(2)}) %all-to-all-start.6) | async-done | bytes 1572896 | tf_op jit(solution)/shard_map/all_to_all | solution.py:191
  830.3 109.1 %reduce-scatter.6.cloned.1.call-done = f32[96,3352]{1,0:T(8,128)} async-done(((f32[768,3352]{1,0:T(8,128)}), f32[96,3352]{1,0:T(8,128)}) %reduce-scatter.6.cloned.1.call-update) | async-done | bytes 1287184 | tf_op jit(solution)/shard_map/reduce_scatter | solution.py:89
  951.1 39.3 %all-reduce.22 = (f32[768]{0:T(1024)}, f32[4,1792]{1,0:T(4,128)}, f32[1792]{0:T(1024)}, f32[24]{0:T(128)}, f32[24]{0:T(128)}, /*index=5*/f32[24]{0:T(128)}, f32[1536]{0:T(1024)}) all-reduce(f32[768]{0:T(1024)S(1)} %get-tuple-element.770, f32[4,1792]{1,0:T(4,128)S(1)} %pad_maximum_fusion.3, ...), channel_id=1, replica_groups=mesh['seq'=4,'fsdp'=8] {'seq','fsdp'}, use_global_device_ids=true, to_apply=%region_26.27 | all-reduce | flops 11336 | bytes 90688 | tf_op jit(solution)/shard_map/psum | solution.py:237
  993.5 15.5 %all-reduce.26.cloned.1.call-done = (f32[96,3352]{1,0:T(8,128)}, f32[192,768]{1,0:T(8,128)}) async-done(((f32[96,3352]{1,0:T(8,128)}, f32[192,768]{1,0:T(8,128)}), (f32[96,3352]{1,0:T(8,128)}, f32[192,768]{1,0:T(8,128)})) %all-reduce.26.cloned.1.call-update) | async-done | bytes 1877008 | tf_op jit(solution)/shard_map/psum | solution.py:95
  (787 shorter events, 567.3 us)
Async XLA Ops:
  7.2 61.8 %all-gather.4.cloned.1.call-start = ((), (), s32[]{:S(2)}) async-start(), calls=%async_computation.11 | async-start | bytes 5971968 | tf_op jit(solution)/shard_map/all_gather | solution.py:112
  7.9 93.1 %all-gather.8.cloned.1.call-start = ((), (), s32[]{:S(2)}) async-start(), calls=%async_computation.13 | async-start | bytes 2654208 | tf_op jit(solution)/shard_map/all_gather | solution.py:113
  11.9 57.1 %copy-start.49 = (f32[512]{0:T(512)}, f32[512]{0:T(512)S(1)}, u32[]{:S(2)}) copy-start(f32[512]{0:T(512)S(1)} %get-tuple-element.881) | copy-start | bytes 6148
  77.1 8.4 all-to-all-start
  86.1 23.5 %all-to-all-start.1 = ((bf16[512,4,384]{2,0,1:T(8,128)(2,1)}), bf16[512,4,384]{2,0,1:T(8,128)(2,1)S(1)}, u32[]{:S(2)}, u32[]{:S(2)}) async-start(bf16[512,4,384]{2,0,1:T(8,128)(2,1)} %copy.303), calls=%async_computation.1 | async-start | bytes 3145728 | tf_op jit(solution)/shard_map/all_to_all | solution.py:132
  89.7 48.4 %all-gather.6.cloned.1.call-start = ((), (), s32[]{:S(2)}) async-start(), calls=%async_computation.12 | async-start | bytes 1310720 | tf_op jit(solution)/shard_map/all_gather | solution.py:136
  109.6 249.5 %all-to-all-start.2 = ((bf16[512,4,384]{2,0,1:T(8,128)(2,1)}), bf16[512,4,384]{2,0,1:T(8,128)(2,1)}, u32[]{:S(2)}, u32[]{:S(2)}) async-start(bf16[512,4,384]{2,0,1:T(8,128)(2,1)} %copy.311), calls=%async_computation.2 | async-start | bytes 3145728 | tf_op jit(solution)/shard_map/all_to_all | solution.py:134
  118.0 245.8 %copy-start = (f32[2048,384]{1,0:T(8,128)}, f32[2048,384]{1,0:T(8,128)S(1)}, u32[]{:S(2)}) copy-start(f32[2048,384]{1,0:T(8,128)S(1)} %get-tuple-element.839) | copy-start | bytes 9437188
  359.1 27.7 %all-to-all-start.4 = ((bf16[512,4,384]{2,0,1:T(8,128)(2,1)}), bf16[512,4,384]{2,0,1:T(8,128)(2,1)}, u32[]{:S(2)}, u32[]{:S(2)}) async-start(bf16[512,4,384]{2,0,1:T(8,128)(2,1)} %bitcast.536), calls=%async_computation.4 | async-start | bytes 3145728 | tf_op jit(solution)/shard_map/all_to_all | solution.py:171
  363.8 436.5 %reduce-scatter.4.cloned.1.call-start = ((), (), s32[]{:S(2)}) async-start(), calls=%async_computation.14 | async-start | bytes 2621440 | tf_op jit(solution)/shard_map/reduce_scatter | solution.py:189
  367.2 19.5 %copy-start.28 = (f32[384]{0:T(512)S(1)}, f32[384]{0:T(512)}, u32[]{:S(2)}) copy-start(f32[384]{0:T(512)} %dynamic_slice.105) | copy-start | bytes 4612
  724.2 106.1 %reduce-scatter.8.cloned.1.call-start = ((), (), s32[]{:S(2)}) async-start(), calls=%async_computation.16 | async-start | bytes 5308416 | tf_op jit(solution)/shard_map/reduce_scatter | solution.py:90
  726.4 31.9 %copy-start.17 = (bf16[1,512,768]{2,1,0:T(8,128)(2,1)S(1)}, bf16[1,512,768]{2,1,0:T(8,128)(2,1)}, u32[]{:S(2)}) copy-start(bf16[1,512,768]{2,1,0:T(8,128)(2,1)} %param.25) | copy-start | bytes 2359300
  763.3 12.6 %all-to-all-start.7 = ((bf16[4,512,6]{1,2,0:T(8,128)(2,1)}), bf16[4,512,6]{1,2,0:T(8,128)(2,1)S(1)}, u32[]{:S(2)}, u32[]{:S(2)}) async-start(bf16[4,512,6]{1,2,0:T(8,128)(2,1)} %fusion.149), calls=%async_computation.8 | async-start | bytes 65536 | tf_op jit(solution)/shard_map/all_to_all | solution.py:192
  775.9 20.4 %all-to-all-start.5 = ((bf16[4,512,384]{1,2,0:T(8,128)(2,1)}), bf16[4,512,384]{1,2,0:T(8,128)(2,1)}, u32[]{:S(2)}, u32[]{:S(2)}) async-start(bf16[4,512,384]{1,2,0:T(8,128)(2,1)} %copy.314), calls=%async_computation.5 | async-start | bytes 3145728 | tf_op jit(solution)/shard_map/all_to_all | solution.py:193
  792.8 26.0 %copy-start.12 = (bf16[1,512,768]{2,1,0:T(8,128)(2,1)S(1)}, bf16[1,512,768]{2,1,0:T(8,128)(2,1)}, u32[]{:S(2)}) copy-start(bf16[1,512,768]{2,1,0:T(8,128)(2,1)} %param.15) | copy-start | bytes 2359300
  792.8 26.0 %copy-start.50 = (f32[512]{0:T(512)S(1)}, f32[512]{0:T(512)}, u32[]{:S(2)}) copy-start(f32[512]{0:T(512)} %copy-done.49) | copy-start | bytes 6148
  792.8 26.0 %copy-start.54 = (f32[768]{0:T(1024)S(1)}, f32[768]{0:T(1024)}, u32[]{:S(2)}) copy-start(f32[768]{0:T(1024)} %param.16) | copy-start | bytes 9220
  796.3 22.5 %all-to-all-start.6 = ((bf16[4,512,384]{1,2,0:T(8,128)(2,1)}), bf16[4,512,384]{1,2,0:T(8,128)(2,1)S(1)}, u32[]{:S(2)}, u32[]{:S(2)}) async-start(bf16[4,512,384]{1,2,0:T(8,128)(2,1)} %copy.324), calls=%async_computation.6 | async-start | bytes 3145728 | tf_op jit(solution)/shard_map/all_to_all | solution.py:191
  800.2 139.3 %reduce-scatter.6.cloned.1.call-start = ((), (), s32[]{:S(2)}) async-start(), calls=%async_computation.15 | async-start | bytes 11943936 | tf_op jit(solution)/shard_map/reduce_scatter | solution.py:89
  828.1 111.3 %copy-start.8 = (bf16[4,512,384]{1,2,0:T(8,128)(2,1)S(1)}, bf16[4,512,384]{1,2,0:T(8,128)(2,1)}, u32[]{:S(2)}) copy-start(bf16[4,512,384]{1,2,0:T(8,128)(2,1)} %copy-done.7) | copy-start | bytes 4718596
  828.2 180.8 %all-reduce.26.cloned.1.call-start = ((), (), s32[]{:S(2)}) async-start(), calls=%async_computation.17 | async-start | bytes 3833856 | tf_op jit(solution)/shard_map/psum | solution.py:95
  943.6 46.8 %copy-start.18 = (bf16[1,512,768]{2,1,0:T(8,128)(2,1)S(1)}, bf16[1,512,768]{2,1,0:T(8,128)(2,1)}, u32[]{:S(2)}) copy-start(bf16[1,512,768]{2,1,0:T(8,128)(2,1)} %param.25) | copy-start | bytes 2359300
  943.6 46.8 %copy-start.48 = (f32[512]{0:T(512)S(1)}, f32[512]{0:T(512)}, u32[]{:S(2)}) copy-start(f32[512]{0:T(512)} %get-tuple-element.880) | copy-start | bytes 6148
  (56 other events, 408.2 us)
Sparse Core Ops, SparseCore 0:
  9.7 59.2 all-gather.3
  70.6 30.3 all-gather.7
  103.4 34.5 all-gather.5
  724.4 46.4 reduce-scatter.3
  773.1 54.9 reduce-scatter.7
  830.4 108.9 reduce-scatter.5
  942.7 66.2 all-reduce.25
where the time goes:
time: 1030 us; the launch traced here: 1020 us
  local copies, waits for them, and re-layouts  320 us (31%)
  waiting for transfers between devices  217 us (21%)
  other arithmetic  175 us (17%)
  matrix products  165 us (16%)
  blocking collectives  96.9 us (9%)
  starting transfers between devices  28.5 us (3%)
  between operations  15.3 us (1%)
    dynamic_update_slice x32, local copies, waits for them, and re-layouts, state_scan(): final_state, outputs = lax.scan(jax.checkpoint(block_step), initial, blocks)  170 us
    reduce_scatter x1, waiting for transfers between devices, fsdp_rows(): lax.psum_scatter(first, 'fsdp', scatter_dimension=0, tiled=True)  109 us
    another operation x73, other arithmetic  104 us
    all_gather x1, waiting for transfers between devices, body(): lax.all_gather(w_in, 'fsdp', axis=0, tiled=True)  57.1 us
    dot_general x24, matrix products, block_step(): within = jnp.einsum('hts,shp->thp', mixing, x_block, precision=precise)  56.5 us
    psum x1, blocking collectives, body(): lax.psum((d_norm_gain, conv_grad, bias_grad, shift_grad, decay_grad, skip...  39.3 us
    unnamed x126, local copies, waits for them, and re-layouts  36.8 us
    all_to_all x1, blocking collectives, body(): lax.all_to_all(normed_head, 'seq', split_axis=0, concat_axis=1, tiled=True)  30.8 us
  transfers between devices with their start and end apart: 14, of which 8 were waited for; matrix products, arithmetic and copies ran while one was open for 32% of the time, Pallas kernels for 0%

commit v1 on v0

v1 whole, which is shorter than its diff:
```python
from functools import partial

import jax
import jax.numpy as jnp
from jax import lax
from jax.sharding import PartitionSpec as P

D = 768
HEADS = 24
HEAD_DIM = 64
STATE = 128
CONVW = 4
CHUNK = 128
INNER = 1536
CONV = INNER + 2 * STATE

epsilon = 1e-05
precise = lax.Precision.HIGHEST
bf16 = jnp.bfloat16
f32 = jnp.float32


@partial(jax.custom_vjp, nondiff_argnums=(0,))
def mm(spec, left, right):
    return jnp.einsum(spec, left.astype(bf16), right.astype(bf16), preferred_element_type=f32)


def mm_keep(spec, left, right):
    left, right = left.astype(bf16), right.astype(bf16)
    return jnp.einsum(spec, left, right, preferred_element_type=f32), (left, right)


def mm_back(spec, kept, grad):
    left, right = kept
    sides, out = spec.split("->")
    one, two = sides.split(",")
    grad = grad.astype(bf16)
    return (
        jnp.einsum(f"{out},{two}->{one}", grad, right, preferred_element_type=f32),
        jnp.einsum(f"{one},{out}->{two}", left, grad, preferred_element_type=f32),
    )


mm.defvjp(mm_keep, mm_back)


def over_heads(values):
    spread = jnp.repeat(jnp.eye(HEADS, dtype=f32), HEAD_DIM, axis=1)
    return jnp.einsum("...h,hk->...k", values, spread, precision=precise)


def shifted(values, by):
    count = lax.axis_size("seq")
    return lax.ppermute(values, "seq", [(at, at + by) for at in range(count - by)])


def incoming(final_state, total):
    sent = final_state.astype(bf16)
    result = shifted(sent, 1).astype(f32)
    gap = 0.0
    for by in range(2, lax.axis_size("seq")):
        gap = gap + shifted(total, by - 1)
        result = result + over_heads(jnp.exp(gap))[None, :] * shifted(sent, by).astype(f32)
    return result


def state_scan(values, b_rows, c_rows, step_size, decay_rates):
    length = values.shape[0]
    chunks = length // CHUNK
    causal = jnp.arange(CHUNK)[:, None] >= jnp.arange(CHUNK)[None, :]
    x_c = values.reshape(chunks, CHUNK, INNER)
    b_c = b_rows.reshape(chunks, CHUNK, STATE)
    c_c = c_rows.reshape(chunks, CHUNK, STATE)
    dt_c = step_size.reshape(chunks, CHUNK, HEADS)
    decay_sum = jnp.einsum(
        "ts,csh->cth", causal.astype(f32), dt_c * decay_rates, precision=precise
    )
    total = decay_sum[:, -1, :]
    remain = jnp.exp(total[:, None, :] - decay_sum) * dt_c
    gains = mm("csn,csk->cnk", b_c, x_c * over_heads(remain))
    whole = over_heads(jnp.exp(total))
    starts = [jnp.zeros((STATE, INNER), f32)]
    for at in range(chunks):
        starts.append(starts[-1] * whole[at][None, :] + gains[at])
    first = incoming(starts[-1], jnp.sum(total, axis=0))
    before = over_heads(jnp.exp(jnp.cumsum(total, axis=0) - total))
    begun = jnp.stack(starts[:-1]) + before[:, None, :] * first[None]
    decay_cols = jnp.swapaxes(decay_sum, 1, 2)
    spread = jnp.where(
        causal[None, None], decay_cols[:, :, :, None] - decay_cols[:, :, None, :], 0.0
    )
    factor = jnp.where(causal[None, None], jnp.exp(spread), 0.0)
    crossing = mm("ctn,csn->cts", c_c, b_c)
    mixing = factor * crossing[:, None] * jnp.swapaxes(dt_c, 1, 2)[:, :, None, :]
    within = mm("chts,chsp->chtp", mixing, jnp.swapaxes(x_c.reshape(chunks, CHUNK, HEADS, HEAD_DIM), 1, 2))
    within = jnp.swapaxes(within, 1, 2).reshape(chunks, CHUNK, INNER)
    earlier = mm("ctn,cnk->ctk", c_c, begun) * over_heads(jnp.exp(decay_sum))
    return (within + earlier).reshape(length, INNER)


def mixer_local(xbc, raw_step, conv_weight, conv_bias, dt_bias, a_log, skip_gain):
    length = xbc.shape[0]
    halo = shifted(xbc[length - CONVW + 1 :].astype(bf16), 1).astype(f32)
    padded = jnp.concatenate([halo, xbc], axis=0)
    summed = conv_bias[None, :]
    for at in range(CONVW):
        summed = summed + conv_weight[at] * padded[at : at + length]
    filtered = jax.nn.silu(summed)
    step_size = jax.nn.softplus(raw_step + dt_bias)
    values = filtered[:, :INNER]
    scanned = state_scan(
        values,
        filtered[:, INNER : INNER + STATE],
        filtered[:, INNER + STATE :],
        step_size,
        -jnp.exp(a_log),
    )
    return scanned + over_heads(skip_gain)[None, :] * values


def plain(left_mat, right_mat):
    return jnp.dot(left_mat, right_mat, preferred_element_type=f32)


def times_transposed(left_mat, right_mat):
    return lax.dot_general(
        left_mat, right_mat, (((1,), (1,)), ((), ())), preferred_element_type=f32
    )


def over_rows(left_mat, right_mat):
    return lax.dot_general(
        left_mat, right_mat, (((0,), (0,)), ((), ())), preferred_element_type=f32
    )


def gathered(rows):
    return lax.all_gather(rows, "fsdp", axis=0, tiled=True)


def reduced(part):
    rows = lax.psum_scatter(part.astype(bf16), "fsdp", scatter_dimension=0, tiled=True)
    return lax.psum(rows, "seq").astype(f32)


def body(
    hidden_in,
    norm_gain,
    w_in,
    conv_weight,
    conv_bias,
    dt_bias,
    a_log,
    skip_gain,
    gate_gain,
    w_out,
    cotangent,
):
    w_scan = gathered(w_in[:, INNER:])
    z_rows, o_rows, w_scan = lax.optimization_barrier((w_in[:, :INNER], w_out, w_scan))
    w_gate = gathered(z_rows)
    w_out_full = gathered(o_rows)
    tokens = hidden_in[0].astype(f32)
    inv_rms = lax.rsqrt(jnp.mean(tokens * tokens, axis=1, keepdims=True) + epsilon)
    normed_in = (tokens * inv_rms * norm_gain).astype(bf16)
    proj_scan = plain(normed_in, w_scan).astype(bf16)
    mixed_raw, mixer_back = jax.vjp(
        mixer_local,
        proj_scan[:, :CONV].astype(f32),
        proj_scan[:, CONV:].astype(f32),
        conv_weight,
        conv_bias,
        dt_bias,
        a_log,
        skip_gain,
    )
    gate_f = plain(normed_in, w_gate).astype(bf16).astype(f32)
    grad_out = cotangent[0]
    d_head = times_transposed(grad_out, w_out_full).astype(bf16).astype(f32)
    mixed_f = lax.optimization_barrier(mixed_raw.astype(bf16)).astype(f32)
    gate_sigmoid = jax.nn.sigmoid(gate_f)
    gate_silu = gate_f * gate_sigmoid
    gated_vals = mixed_f * gate_silu
    gate_rms = lax.rsqrt(jnp.mean(gated_vals * gated_vals, axis=1, keepdims=True) + epsilon)
    normed_out = (gated_vals * gate_rms * gate_gain).astype(bf16)
    d_w_out_part = over_rows(normed_out, grad_out)
    cross = jnp.mean(d_head * gate_gain * gated_vals, axis=1, keepdims=True)
    gain_grad = jnp.sum(d_head * gated_vals * gate_rms, axis=0)
    d_gated = gate_rms * gate_gain * d_head - gated_vals * gate_rms**3 * cross
    d_mixed = lax.optimization_barrier((d_gated * gate_silu).astype(bf16)).astype(f32)
    d_gate = (d_gated * mixed_f * gate_sigmoid * (1.0 + gate_f * (1.0 - gate_sigmoid))).astype(
        bf16
    )
    d_w_gate_part = over_rows(normed_in, d_gate)
    grad_w_out = reduced(d_w_out_part)
    grad_w_gate = reduced(d_w_gate_part)
    result = (tokens + plain(normed_out, w_out_full)).astype(bf16)
    d_xbc, d_step, conv_grad, bias_grad, shift_grad, decay_grad, skip_grad = mixer_back(d_mixed)
    d_scan = jnp.concatenate([d_xbc, d_step], axis=1).astype(bf16)
    grad_w_scan = reduced(over_rows(normed_in, d_scan))
    d_normed_in = times_transposed(d_gate, w_gate) + times_transposed(d_scan, w_scan)
    norm_gain_grad = jnp.sum(d_normed_in * tokens * inv_rms, axis=0)
    norm_cross = jnp.sum(d_normed_in * norm_gain * tokens, axis=1, keepdims=True)
    d_tokens = (
        inv_rms * norm_gain * d_normed_in
        - tokens * inv_rms**3 * norm_cross / D
        + grad_out.astype(f32)
    )
    small = (
        norm_gain_grad,
        conv_grad,
        bias_grad,
        shift_grad,
        decay_grad,
        skip_grad,
        gain_grad,
    )
    flat = lax.psum(jnp.concatenate([each.reshape(-1) for each in small]), ("seq", "fsdp"))
    sums, at = [], 0
    for each in small:
        sums.append(flat[at : at + each.size].reshape(each.shape))
        at += each.size
    return (
        result[None],
        d_tokens[None],
        sums[0],
        jnp.concatenate([grad_w_gate, grad_w_scan], axis=1),
        sums[1],
        sums[2],
        sums[3],
        sums[4],
        sums[5],
        sums[6],
        grad_w_out,
    )


def solution(mesh):
    rows = P("fsdp", None)
    part = P("fsdp", "seq", None)
    return jax.shard_map(
        body,
        mesh=mesh,
        in_specs=(part, P(), rows, P(), P(), P(), P(), P(), P(), rows, part),
        out_specs=(part, part, P(), rows, P(), P(), P(), P(), P(), P(), rows),
        check_vma=False,
    )
```

time: 1030 us -> 390 us (0.38)
  local copies, waits for them, and re-layouts: 320 us -> 50.2 us
  waiting for transfers between devices: 217 us -> 84.2 us
  other arithmetic: 175 us -> 76.4 us
  matrix products: 165 us -> 92.7 us
  blocking collectives: 96.9 us -> 38.5 us
    dynamic_update_slice x36 -> x0, local copies, waits for them, and re-layouts: 171 us -> none  [the longest x32 170 us: state_scan(): final_state, outputs = lax.scan(jax.checkpoint(block_step), initial, blocks)]
    another operation x81 -> x4, other arithmetic: 104 us -> 13.5 us
    reduce_scatter x3, waiting for transfers between devices: 109 us -> 31.5 us  [reduced(): lax.psum_scatter(part.astype(bf16), 'fsdp', scatter_dimension=0, tiled=True)]
    dot_general x114 -> x31, matrix products: 142 us -> 64.6 us  [the longest x14 23 us: over_heads(): return jnp.einsum('...h,hk->...k', values, spread, precision=precise)]
    all_to_all x1 -> x0, blocking collectives: 30.8 us -> none  [body(): lax.all_to_all(normed_head, 'seq', split_axis=0, concat_axis=1, tiled=True)]
    all_gather x3, waiting for transfers between devices: 69 us -> 38.8 us  [gathered(): return lax.all_gather(rows, 'fsdp', axis=0, tiled=True)]
    squeeze x32 -> x0, local copies, waits for them, and re-layouts: 29.7 us -> none  [state_scan(): final_state, outputs = lax.scan(jax.checkpoint(block_step), initial, blocks)]
    unnamed x126 -> x211, local copies, waits for them, and re-layouts: 36.8 us -> 7.61 us
  transfers between devices with their start and end apart: 14 -> 19, of which waited for: 8 -> 5; matrix products, arithmetic and copies ran while one was open for 32% -> 49% of each run, Pallas kernels for 0% -> 0%
where the time goes in v1:
time: 390 us; the launch traced here: 384 us
  matrix products  92.7 us (24%)
  waiting for transfers between devices  84.2 us (22%)
  other arithmetic  76.4 us (20%)
  local copies, waits for them, and re-layouts  50.2 us (13%)
  blocking collectives  38.5 us (10%)
  starting transfers between devices  25.8 us (7%)
  between operations  15.8 us (4%)
    all_gather x3, waiting for transfers between devices, gathered(): return lax.all_gather(rows, 'fsdp', axis=0, tiled=True)  38.8 us
    psum x1, blocking collectives, body(): lax.psum(jnp.concatenate([each.reshape(-1) for each in small]), ('seq', '...  38.5 us
    reduce_scatter x3, waiting for transfers between devices, reduced(): lax.psum_scatter(part.astype(bf16), 'fsdp', scatter_dimension=0, tiled=True)  31.5 us
    ppermute x12, starting transfers between devices, shifted(): lax.ppermute(values, 'seq', [(at, at + by) for at in range(count - by)])  24.9 us
    dot_general x14, matrix products, over_heads(): return jnp.einsum('...h,hk->...k', values, spread, precision=precise)  23 us
    dot_general x3, matrix products, times_transposed(): lax.dot_general(left_mat, right_mat, (((1,), (1,)), ((), ())), preferred_...  16.2 us
    another operation x2, other arithmetic  12.8 us
    dot_general x3, matrix products, over_rows(): lax.dot_general(left_mat, right_mat, (((0,), (0,)), ((), ())), preferred_...  12 us
  transfers between devices with their start and end apart: 19, of which 5 were waited for; matrix products, arithmetic and copies ran while one was open for 49% of the time, Pallas kernels for 0%

profile of v1, /device:TPU:0, one launch (start us, length us, event | category | flops | bytes accessed | tf_op | source)
XLA Modules:
  0.0 383.7 jit_solution(11366100949638744272)
XLA Ops:
  10.9 38.8 %all-gather.4.cloned.1.call-done = bf16[768,1816]{1,0:T(8,128)(2,1)} async-done(((bf16[96,1816]{1,0:T(8,128)(2,1)}), bf16[768,1816]{1,0:T(8,128)(2,1)}) %all-gather.4.cloned.1.call-update) | async-done | bytes 2789392 | tf_op jit(solution)/shard_map/all_gather | solution.py:138
  68.9 4.4 %fusion.119 = f32[4,128,1536]{2,1,0:T(8,128)} fusion(f32[24,1536,1]{1,0,2:T(8,128)S(1)} %reshape.302, f32[4,24,128]{2,1,0:T(8,128)S(1)} %fusion.109), kind=kOutput, calls=%fused_computation.220 | convolution fusion | flops 226492416 | bytes 3342336 | tf_op jit(solution)/shard_map/jvp(...h,hk->...k)/dot_general | solution.py:49
  77.9 12.0 %fusion.159 = (bf16[512,1792]{0,1:T(8,128)(2,1)S(1)}, f32[512,1792]{0,1:T(8,128)S(1)}, f32[512,1792]{0,1:T(8,128)}) fusion(f32[512,1792]{0,1:T(8,128)} %slice_convert_fusion, f32[1792]{0:T(1024)S(1)} %get-tuple-element.45, f32[3,1792]{0,1:T(8,128)S(1)} %convert_element_type.188, f32[1792]{0:T(1024)S(1)} %get-tuple-element.46, ...), kind=kLoop, calls=%fused_computation.271 | loop fusion | flops 14680064 | bytes 12902400 | tf_op jit(solution)/shard_map/convert.9
  96.6 4.6 %multiply_convert_fusion.4 = (bf16[4,128,1536]{2,1,0:T(8,128)(2,1)S(1)}, f32[4,128,1536]{2,1,0:T(8,128)}) fusion(f32[4,128,1536]{2,1,0:T(8,128)S(1)} %bitcast.277, f32[24,1536,1]{1,0,2:T(8,128)S(1)} %reshape.302, f32[3,4,8,128]{3,2,1,0:T(8,128)S(1)} %get-tuple-element.75, f32[4,24]{1,0:T(4,128)S(1)} %slice_reduce_fusion.1, f32[4,24,128]{2,1,0:T(8,128)S(1)} %fusion.109), kind=kOutput, calls=%fused_computation.76 | convolution fusion | flops 228089856 | bytes 8110464 | tf_op jit(solution)/shard_map/jvp(...h,hk->...k)/dot_general | solution.py:49
  116.1 5.3 %fusion.28 = f32[4,24,128,64]{2,3,1,0:T(8,128)} fusion(f32[4,24,128]{2,1,0:T(8,128)} %copy.85, f32[4,128,128]{2,1,0:T(8,128)} %fusion.88, f32[4,24,128]{2,1,0:T(8,128)S(1)} %fusion.109, pred[128,128]{1,0:T(8,128)(4,1)} %iota_compare_fusion, bf16[4,128,24,64]{1,0,3,2:T(4,128)(2,1)} %convert_element_type.194), kind=kOutput, calls=%fused_computation.81 | convolution fusion | flops 210763776 | bytes 5095424 | tf_op jit(solution)/shard_map/jvp(chts,chsp->chtp)/dot_general | solution.py:30
  136.5 4.3 %add_convert_fusion.1 = bf16[512,1536]{0,1:T(8,128)(2,1)} fusion(f32[512,1536]{0,1:T(8,128)} %copy.114, f32[1536]{0:T(1024)} %convolution_reduce_fusion, f32[512,1792]{0,1:T(8,128)} %copy-done.2), kind=kLoop, calls=%fused_computation.74 | loop fusion | flops 2359296 | bytes 7870464 | tf_op jit(solution)/shard_map/convert_element_type | solution.py:180
  140.9 4.8 %multiply_reduce_fusion.9 = (f32[512]{0:T(512)S(1)}, bf16[512,1536]{0,1:T(8,128)(2,1)S(1)}) fusion(bf16[512,1536]{0,1:T(8,128)(2,1)} %add_convert_fusion.1, bf16[768,1536]{1,0:T(8,128)(2,1)} %all-gather.6.cloned.1.call-done, bf16[1,512,768]{2,1,0:T(8,128)(2,1)} %param.11, f32[768]{0:T(1024)} %param.12, f32[512]{0:T(512)} %copy-done.83), kind=kOutput, calls=%fused_computation.73 | convolution fusion | flops 1217396224 | bytes 6298624 | tf_op jit(solution)/shard_map/dot_general | solution.py:122
  150.6 6.3 %fusion.22 = (f32[1536]{0:T(1024)}, f32[512]{0:T(512)S(1)}, bf16[1536,512]{1,0:T(8,128)(2,1)S(1)}) fusion(f32[512]{0:T(512)} %copy-done.85, bf16[512,1536]{0,1:T(8,128)(2,1)} %copy-done.41, bf16[512,1536]{0,1:T(8,128)(2,1)} %add_convert_fusion.1, f32[1536]{0:T(1024)} %param.19, bf16[1536,768]{1,0:T(8,128)(2,1)} %all-gather.8.cloned.1.call-done, ...), kind=kOutput, calls=%fused_computation.59 | convolution fusion | flops 1219753984 | bytes 7880704 | tf_op jit(solution)/shard_map/dot_general | solution.py:126
  156.9 4.0 %multiply_convert_fusion.2 = (bf16[512,1536]{0,1:T(8,128)(2,1)}, bf16[512,1536]{0,1:T(8,128)(2,1)}) fusion(bf16[512,1536]{0,1:T(8,128)(2,1)S(1)} %copy-done.42, f32[512]{0:T(512)S(1)} %broadcast_multiply_fusion.4, f32[512]{0:T(512)S(1)} %copy-done.88, bf16[1536,512]{1,0:T(8,128)(2,1)S(1)} %get-tuple-element.99, f32[1536]{0:T(1024)S(1)} %copy-done.78, ...), kind=kLoop, calls=%fused_computation.71 | loop fusion | flops 17301504 | bytes 7876608 | tf_op jit(solution)/shard_map/convert_element_type | solution.py:190
  182.5 7.3 %fusion.9 = (f32[4,24,128]{2,1,0:T(8,128)}, f32[4,24,128]{2,1,0:T(8,128)}, f32[4,24,128]{2,1,0:T(8,128)}, bf16[4,128,128]{2,1,0:T(8,128)(2,1)S(1)}) fusion(f32[4,24,128]{2,1,0:T(8,128)S(1)} %copy-done.70, f32[4,128,128]{2,1,0:T(8,128)S(1)} %copy-done.47, f32[4,24,128]{2,1,0:T(8,128)S(1)} %fusion.109, pred[128,128]{1,0:T(8,128)(4,1)S(1)} %copy-done.75, ...), kind=kOutput, calls=%fused_computation.42 | convolution fusion | flops 224817152 | bytes 3801088 | tf_op jit(solution)/shard_map/transpose(jvp(chtp,chsp->chts))/dot_general | solution.py:95
  192.5 3.8 fusion.27
  205.1 4.7 %convolution_convert_fusion.2 = bf16[768,1536]{1,0:T(8,128)(2,1)} fusion(bf16[512,1536]{0,1:T(8,128)(2,1)} %get-tuple-element.68, bf16[1,512,768]{2,1,0:T(8,128)(2,1)} %param.11, f32[768]{0:T(1024)} %param.12, f32[512]{0:T(512)} %copy-done.83), kind=kOutput, calls=%fused_computation.40 | convolution fusion | flops 1210712064 | bytes 4723712 | tf_op jit(solution)/shard_map/dot_general | solution.py:132
  224.3 4.0 %copy.117 = f32[512,1536]{0,1:T(8,128)} copy(f32[512,1536]{1,0:T(8,128)} %bitcast.282) | data formatting | bytes 6291456 | tf_op jit(solution)/shard_map/transpose(jvp())/reshape | solution.py:71
  229.5 4.6 %multiply_reduce_fusion.6 = (f32[1536]{0:T(1024)}, f32[512,1536]{0,1:T(8,128)S(1)}) fusion(bf16[512,1536]{0,1:T(8,128)(2,1)S(1)} %copy-done.8, f32[512,1792]{0,1:T(8,128)} %copy-done.2, f32[512,1536]{0,1:T(8,128)} %copy.117, f32[1536]{0:T(1024)S(1)} %copy-done.66), kind=kLoop, calls=%fused_computation.60 | loop fusion | flops 3930624 | bytes 11022336 | tf_op jit(solution)/shard_map/transpose(jvp())/reduce_sum | solution.py:118
  234.8 9.1 %multiply_reduce_fusion.4 = (f32[1792]{0:T(1024)S(1)}, f32[1792]{0:T(1024)S(1)}, f32[1792]{0:T(1024)S(1)}, f32[1792]{0:T(1024)S(1)}, f32[1792]{0:T(1024)S(1)}, /*index=5*/f32[512,1792]{0,1:T(8,128)S(1)}) fusion(f32[512,1792]{0,1:T(8,128)S(1)} %copy-done.3, f32[3,1792]{0,1:T(8,128)S(1)} %copy-done.16, bf16[512,1816]{0,1:T(8,128)(2,1)} %copy-done.14, ...), kind=kLoop, calls=%fused_computation.27 | loop fusion | flops 22011136 | bytes 16572416 | tf_op jit(solution)/shard_map/transpose(jvp())/reduce_sum | solution.py:107
  244.0 4.7 %broadcast_multiply_fusion = (f32[512,1792]{0,1:T(8,128)S(1)}, f32[512,1792]{0,1:T(8,128)}, f32[512,1792]{0,1:T(8,128)}, f32[512,1792]{0,1:T(8,128)}) fusion(f32[512,1792]{0,1:T(8,128)S(1)} %get-tuple-element.56, f32[1792]{0:T(1024)S(1)} %copy-done.61, f32[1792]{0:T(1024)S(1)} %copy-done.57, f32[1792]{0:T(1024)S(1)} %copy-done.59, f32[1792]{0:T(1024)S(1)} %copy-done.63), kind=kLoop, calls=%fused_computation.84 | loop fusion | flops 3670016 | bytes 18378752 | tf_op jit(solution)/shard_map/transpose(jvp())/mul | solution.py:107
  248.7 8.3 %pad_add_fusion = f32[515,1792]{0,1:T(8,128)S(1)} fusion(f32[512,1792]{0,1:T(8,128)} %get-tuple-element.70, f32[512,1792]{0,1:T(8,128)} %get-tuple-element.71, f32[512,1792]{0,1:T(8,128)} %get-tuple-element.72, f32[512,1792]{0,1:T(8,128)S(1)} %get-tuple-element.69), kind=kLoop, calls=%fused_computation.15 | loop fusion | flops 2768640 | bytes 18371584 | tf_op jit(solution)/shard_map/transpose(jvp())/add_any | solution.py:107
  258.6 4.9 %fusion.63 = f32[4,24,128]{2,1,0:T(8,128)S(1)} fusion(f32[24,1536,1]{1,0,2:T(8,128)S(1)} %reshape.302, f32[4,128,1536]{2,1,0:T(8,128)} %get-tuple-element.96, f32[4,128,1536]{2,1,0:T(8,128)S(1)} %bitcast.280, f32[4,1,24]{1,2,0:T(8,128)S(1)} %copy-done.51, f32[4,24,128]{2,1,0:T(8,128)S(1)} %copy-done.68, f32[4,24,128]{2,1,0:T(8,128)S(1)} %copy-done.67, ...), kind=kOutput, calls=%fused_computation.121 | convolution fusion | flops 227401728 | bytes 6734592 | tf_op jit(solution)/shard_map/transpose(jvp(...h,hk->...k))/dot_general | solution.py:49
  264.9 6.4 %collective-permute-done.9 = bf16[3,1792]{0,1:T(8,128)(2,1)S(1)} collective-permute-done((bf16[3,1792]{0,1:T(8,128)(2,1)S(1)}, bf16[3,1792]{0,1:T(8,128)(2,1)S(1)}, u32[]{:S(2)}, u32[]{:S(2)}) %collective-permute-start.9) | collective-permute-done | bytes 10784 | tf_op jit(solution)/shard_map/transpose(jvp())/ppermute | solution.py:54
  277.2 4.9 %fusion.166 = f32[512,768]{1,0:T(8,128)} fusion(bf16[512,1536]{0,1:T(8,128)(2,1)} %get-tuple-element.68, bf16[768,1536]{1,0:T(8,128)(2,1)} %all-gather.6.cloned.1.call-done), kind=kOutput, calls=%fused_computation.275 | convolution fusion | flops 1207959552 | bytes 5505024 | tf_op jit(solution)/shard_map/dot_general | solution.py:126
  285.6 31.4 %reduce-scatter.6.cloned.1.call-done = bf16[96,1816]{1,0:T(8,128)(2,1)} async-done(((bf16[768,1816]{1,0:T(8,128)(2,1)}), bf16[96,1816]{1,0:T(8,128)(2,1)}) %reduce-scatter.6.cloned.1.call-update) | async-done | bytes 348688 | tf_op jit(solution)/shard_map/reduce_scatter | solution.py:142
  317.1 5.0 %fusion.40 = (f32[768]{0:T(1024)S(1)}, f32[512]{0:T(512)S(1)}, f32[512,768]{1,0:T(8,128)S(1)}) fusion(bf16[1,512,768]{2,1,0:T(8,128)(2,1)S(1)} %copy-done.37, f32[512]{0:T(512)S(1)} %copy-done.84, f32[768]{0:T(1024)S(1)} %copy-done.92, f32[512,768]{1,0:T(8,128)} %fusion.166, bf16[768,1816]{1,0:T(8,128)(2,1)} %all-gather.4.cloned.1.call-done, ...), kind=kOutput, calls=%fused_computation.99 | convolution fusion | flops 1435024128 | bytes 8591360 | tf_op jit(solution)/shard_map/dot_general | solution.py:126
  322.2 38.5 %psum.28 = f32[11336]{0:T(1024)S(1)} all-reduce(f32[11336]{0:T(1024)S(1)} %concatenate.18), channel_id=1, replica_groups=mesh['seq'=4,'fsdp'=8] {'seq','fsdp'}, use_global_device_ids=true, to_apply=%region_30.31 | all-reduce | flops 11336 | bytes 90688 | tf_op jit(solution)/shard_map/psum | solution.py:218
  365.5 7.0 %all-reduce.24.cloned.1.call-done = (bf16[96,1816]{1,0:T(8,128)(2,1)}, bf16[96,1536]{1,0:T(8,128)(2,1)}, bf16[192,768]{1,0:T(8,128)(2,1)}) async-done(((bf16[96,1816]{1,0:T(8,128)(2,1)}, bf16[96,1536]{1,0:T(8,128)(2,1)}, bf16[192,768]{1,0:T(8,128)(2,1)}), (bf16[96,1816]{1,0:T(8,128)(2,1)}, bf16[96,1536]{1,0:T(8,128)(2,1)}, bf16[192,768]{1,0:T(8,128)(2,1)})) %all-reduce.24.cloned.1.call-update) | async-done | bytes 938512 | tf_op jit(solution)/shard_map/psum | solution.py:143
  (352 shorter events, 138.5 us)
Async XLA Ops:
  7.2 45.3 %copy-start.103 = (f32[24]{0:T(128)S(1)}, f32[24]{0:T(128)}, u32[]{:S(2)}) copy-start(f32[24]{0:T(128)} %param.17) | copy-start | bytes 292
  7.2 45.9 %copy-start.91 = (f32[768]{0:T(1024)S(1)}, f32[768]{0:T(1024)}, u32[]{:S(2)}) copy-start(f32[768]{0:T(1024)} %param.12) | copy-start | bytes 9220
  7.2 42.5 %all-gather.4.cloned.1.call-start = ((), (), s32[]{:S(2)}) async-start(), calls=%async_computation.3 | async-start | bytes 3317760 | tf_op jit(solution)/shard_map/all_gather | solution.py:138
  9.1 131.7 %all-gather.6.cloned.1.call-start = ((), (), s32[]{:S(2)}) async-start(), calls=%async_computation.4 | async-start | bytes 2654208 | tf_op jit(solution)/shard_map/all_gather | solution.py:138
  49.7 100.8 %all-gather.8.cloned.1.call-start = ((), (), s32[]{:S(2)}) async-start(), calls=%async_computation.5 | async-start | bytes 2654208 | tf_op jit(solution)/shard_map/all_gather | solution.py:138
  57.6 18.4 %collective-permute-start.4 = (f32[24]{0:T(128)S(1)}, f32[24]{0:T(128)S(1)}, u32[]{:S(2)}, u32[]{:S(2)}) collective-permute-start(f32[24]{0:T(128)S(1)} %get-tuple-element.41), channel_id=1, source_target_pairs={{0,16},{8,24},{1,17},{9,25},{2,18},{10,26},{3,19},{11,27},{4,20},{... | collective-permute-start | bytes 296 | tf_op jit(solution)/shard_map/jvp()/ppermute | solution.py:54
  61.0 15.1 %collective-permute-start.2 = (f32[24]{0:T(128)S(1)}, f32[24]{0:T(128)S(1)}, u32[]{:S(2)}, u32[]{:S(2)}) collective-permute-start(f32[24]{0:T(128)S(1)} %get-tuple-element.41), channel_id=1, source_target_pairs={{0,8},{8,16},{16,24},{1,9},{9,17},{17,25},{2,10},{10,18},{18,26},{... | collective-permute-start | bytes 296 | tf_op jit(solution)/shard_map/jvp()/ppermute | solution.py:54
  65.2 12.5 %collective-permute-start = (bf16[3,1792]{0,1:T(8,128)(2,1)S(1)}, bf16[3,1792]{0,1:T(8,128)(2,1)S(1)}, u32[]{:S(2)}, u32[]{:S(2)}) collective-permute-start(bf16[3,1792]{0,1:T(8,128)(2,1)S(1)} %slice.129), channel_id=1, source_target_pairs={{0,8},{8,16},{16,24},{1,9},{9,17},{17,25},{2,10},{10,18},{18,26},{... | collective-permute-start | bytes 32264 | tf_op jit(solution)/shard_map/jvp()/ppermute | solution.py:54
  75.6 210.0 %reduce-scatter.8.cloned.1.call-start = ((), (), s32[]{:S(2)}) async-start(), calls=%async_computation.8 | async-start | bytes 2654208 | tf_op jit(solution)/shard_map/reduce_scatter | solution.py:142
  76.1 100.1 %copy-start.80 = (f32[24]{0:T(128)}, f32[24]{0:T(128)S(1)}, u32[]{:S(2)}) copy-start(f32[24]{0:T(128)S(1)} %collective-permute-done.2) | copy-start | bytes 292
  103.4 22.9 %collective-permute-start.5 = (bf16[128,1536]{1,0:T(8,128)(2,1)}, bf16[128,1536]{1,0:T(8,128)(2,1)}, u32[]{:S(2)}, u32[]{:S(2)}) collective-permute-start(bf16[128,1536]{1,0:T(8,128)(2,1)} %get-tuple-element.59), channel_id=1, source_target_pairs={{0,24},{1,25},{2,26},{3,27},{4,28},{5,29},{6,30},{7,31}} | collective-permute-start | bytes 1179656 | tf_op jit(solution)/shard_map/jvp()/ppermute | solution.py:54
  106.9 19.4 %collective-permute-start.3 = (bf16[128,1536]{1,0:T(8,128)(2,1)}, bf16[128,1536]{1,0:T(8,128)(2,1)}, u32[]{:S(2)}, u32[]{:S(2)}) collective-permute-start(bf16[128,1536]{1,0:T(8,128)(2,1)} %get-tuple-element.59), channel_id=1, source_target_pairs={{0,16},{8,24},{1,17},{9,25},{2,18},{10,26},{3,19},{11,27},{4,20},{... | collective-permute-start | bytes 1179656 | tf_op jit(solution)/shard_map/jvp()/ppermute | solution.py:54
  109.5 16.8 %collective-permute-start.1 = (bf16[128,1536]{1,0:T(8,128)(2,1)}, bf16[128,1536]{1,0:T(8,128)(2,1)}, u32[]{:S(2)}, u32[]{:S(2)}) collective-permute-start(bf16[128,1536]{1,0:T(8,128)(2,1)} %get-tuple-element.59), channel_id=1, source_target_pairs={{0,8},{8,16},{16,24},{1,9},{9,17},{17,25},{2,10},{10,18},{18,26},{... | collective-permute-start | bytes 1179656 | tf_op jit(solution)/shard_map/jvp()/ppermute | solution.py:54
  167.4 118.2 %reduce-scatter.4.cloned.1.call-start = ((), (), s32[]{:S(2)}) async-start(), calls=%async_computation.6 | async-start | bytes 2654208 | tf_op jit(solution)/shard_map/reduce_scatter | solution.py:142
  177.0 33.2 %collective-permute-start.10 = (f32[24]{0:T(128)}, f32[24]{0:T(128)}, u32[]{:S(2)}, u32[]{:S(2)}) collective-permute-start(f32[24]{0:T(128)} %fusion.66), channel_id=1, source_target_pairs={{16,0},{24,8},{17,1},{25,9},{18,2},{26,10},{19,3},{27,11},{20,4},{... | collective-permute-start | bytes 296 | tf_op jit(solution)/shard_map/transpose(jvp())/ppermute | solution.py:54
  178.3 33.0 %collective-permute-start.8 = (bf16[128,1536]{1,0:T(8,128)(2,1)}, bf16[128,1536]{1,0:T(8,128)(2,1)}, u32[]{:S(2)}, u32[]{:S(2)}) collective-permute-start(bf16[128,1536]{1,0:T(8,128)(2,1)} %get-tuple-element.81), channel_id=1, source_target_pairs={{8,0},{16,8},{24,16},{9,1},{17,9},{25,17},{10,2},{18,10},{26,18},{... | collective-permute-start | bytes 1179656 | tf_op jit(solution)/shard_map/transpose(jvp())/ppermute | solution.py:54
  179.6 31.7 %collective-permute-start.7 = (bf16[128,1536]{1,0:T(8,128)(2,1)}, bf16[128,1536]{1,0:T(8,128)(2,1)}, u32[]{:S(2)}, u32[]{:S(2)}) collective-permute-start(bf16[128,1536]{1,0:T(8,128)(2,1)} %get-tuple-element.82), channel_id=1, source_target_pairs={{16,0},{24,8},{17,1},{25,9},{18,2},{26,10},{19,3},{27,11},{20,4},{... | collective-permute-start | bytes 1179656 | tf_op jit(solution)/shard_map/transpose(jvp())/ppermute | solution.py:54
  180.9 30.4 %collective-permute-start.6 = (bf16[128,1536]{1,0:T(8,128)(2,1)}, bf16[128,1536]{1,0:T(8,128)(2,1)}, u32[]{:S(2)}, u32[]{:S(2)}) collective-permute-start(bf16[128,1536]{1,0:T(8,128)(2,1)} %get-tuple-element.83), channel_id=1, source_target_pairs={{24,0},{25,1},{26,2},{27,3},{28,4},{29,5},{30,6},{31,7}} | collective-permute-start | bytes 1179656 | tf_op jit(solution)/shard_map/transpose(jvp())/ppermute | solution.py:54
  203.8 6.4 %collective-permute-start.11 = (f32[24]{0:T(128)}, f32[24]{0:T(128)}, u32[]{:S(2)}, u32[]{:S(2)}) collective-permute-start(f32[24]{0:T(128)} %fusion.68), channel_id=1, source_target_pairs={{8,0},{16,8},{24,16},{9,1},{17,9},{25,17},{10,2},{18,10},{26,18},{... | collective-permute-start | bytes 296 | tf_op jit(solution)/shard_map/transpose(jvp())/ppermute | solution.py:54
  209.8 107.2 %reduce-scatter.6.cloned.1.call-start = ((), (), s32[]{:S(2)}) async-start(), calls=%async_computation.7 | async-start | bytes 3317760 | tf_op jit(solution)/shard_map/reduce_scatter | solution.py:142
  257.1 14.3 %collective-permute-start.9 = (bf16[3,1792]{0,1:T(8,128)(2,1)S(1)}, bf16[3,1792]{0,1:T(8,128)(2,1)S(1)}, u32[]{:S(2)}, u32[]{:S(2)}) collective-permute-start(bf16[3,1792]{0,1:T(8,128)(2,1)S(1)} %split.15), channel_id=1, source_target_pairs={{8,0},{16,8},{24,16},{9,1},{17,9},{25,17},{10,2},{18,10},{26,18},{... | collective-permute-start | bytes 32264 | tf_op jit(solution)/shard_map/transpose(jvp())/ppermute | solution.py:54
  277.2 95.4 %all-reduce.24.cloned.1.call-start = ((), (), s32[]{:S(2)}) async-start(), calls=%async_computation.9 | async-start | bytes 1916928 | tf_op jit(solution)/shard_map/psum | solution.py:143
  317.1 46.8 %copy-start.46 = (bf16[1,512,768]{2,1,0:T(8,128)(2,1)S(1)}, bf16[1,512,768]{2,1,0:T(8,128)(2,1)}, u32[]{:S(2)}) copy-start(bf16[1,512,768]{2,1,0:T(8,128)(2,1)} %param.21) | copy-start | bytes 2359300
  317.1 46.8 %copy-start.82 = (f32[512]{0:T(512)S(1)}, f32[512]{0:T(512)}, u32[]{:S(2)}) copy-start(f32[512]{0:T(512)} %get-tuple-element.89) | copy-start | bytes 6148
  (100 other events, 799.7 us)
Sparse Core Ops, SparseCore 0:
  10.3 39.3 all-gather.3
  51.3 30.4 all-gather.5
  83.5 30.7 all-gather.7
  167.5 33.3 reduce-scatter.7
  210.0 40.6 reduce-scatter.3
  277.2 39.7 reduce-scatter.5
  320.8 51.7 all-reduce.23

commit v2 on v1

--- a/solution.py
+++ b/solution.py
@@ -138,9 +138,19 @@
     return lax.all_gather(rows, "fsdp", axis=0, tiled=True)
 
 
+def seq_total(rows):
+    count = lax.axis_size("seq")
+    terms = [rows.astype(f32)]
+    for other in range(1, count):
+        terms.append(lax.ppermute(rows, "seq", [(at, at ^ other) for at in range(count)]).astype(f32))
+    while len(terms) > 1:
+        terms = [one + two for one, two in zip(terms[::2], terms[1::2])]
+    return terms[0]
+
+
 def reduced(part):
     rows = lax.psum_scatter(part.astype(bf16), "fsdp", scatter_dimension=0, tiled=True)
-    return lax.psum(rows, "seq").astype(f32)
+    return seq_total(rows)
 
 
 def body(

time: 390 us -> 409 us (1.049)
  starting transfers between devices: 25.8 us -> 39.2 us
  matrix products: 92.7 us -> 103 us
  waiting for transfers between devices: 84.2 us -> 79.6 us
    reduce_scatter x3, waiting for transfers between devices: 31.5 us -> 0.01 us  [reduced(): lax.psum_scatter(part.astype(bf16), 'fsdp', scatter_dimension=0, tiled=True)]
    ppermute x0 -> x9, waiting for transfers between devices: none -> 28.5 us  [seq_total(): lax.ppermute(rows, 'seq', [(at, at ^ other) for at in range(count)])]
    ppermute x0 -> x9, starting transfers between devices: none -> 13.4 us  [seq_total(): lax.ppermute(rows, 'seq', [(at, at ^ other) for at in range(count)])]
    psum x1 -> x0, waiting for transfers between devices: 7.04 us -> none  [reduced(): return lax.psum(rows, 'seq').astype(f32)]
    ppermute x12, waiting for transfers between devices: 6.74 us -> 12.1 us  [shifted(): lax.ppermute(values, 'seq', [(at, at + by) for at in range(count - by)])]
  transfers between devices with their start and end apart: 19 -> 27, of which waited for: 5 -> 10; matrix products, arithmetic and copies ran while one was open for 49% -> 47% of each run, Pallas kernels for 0% -> 0%
where the time goes in v2:
time: 409 us; the launch traced here: 403 us
  matrix products  103 us (25%)
  waiting for transfers between devices  79.6 us (19%)
  other arithmetic  74.9 us (18%)
  local copies, waits for them, and re-layouts  50.4 us (12%)
  blocking collectives  40.2 us (10%)
  starting transfers between devices  39.2 us (10%)
  between operations  15.7 us (4%)
    psum x1, blocking collectives, body(): lax.psum(jnp.concatenate([each.reshape(-1) for each in small]), ('seq', '...  40.2 us
    all_gather x3, waiting for transfers between devices, gathered(): return lax.all_gather(rows, 'fsdp', axis=0, tiled=True)  38.8 us
    ppermute x9, waiting for transfers between devices, seq_total(): lax.ppermute(rows, 'seq', [(at, at ^ other) for at in range(count)])  28.5 us
    ppermute x12, starting transfers between devices, shifted(): lax.ppermute(values, 'seq', [(at, at + by) for at in range(count - by)])  25.2 us
    dot_general x14, matrix products, over_heads(): return jnp.einsum('...h,hk->...k', values, spread, precision=precise)  23.8 us
    dot_general x3, matrix products, times_transposed(): lax.dot_general(left_mat, right_mat, (((1,), (1,)), ((), ())), preferred_...  16.7 us
    dot_general x3, matrix products, over_rows(): lax.dot_general(left_mat, right_mat, (((0,), (0,)), ((), ())), preferred_...  14.2 us
    dot_general x2, matrix products, state_scan(): mm('chts,chsp->chtp', mixing, jnp.swapaxes(x_c.reshape(chunks, CHUNK, HEA...  13.6 us
  transfers between devices with their start and end apart: 27, of which 10 were waited for; matrix products, arithmetic and copies ran while one was open for 47% of the time, Pallas kernels for 0%

profile of v2, /device:TPU:0, one launch (start us, length us, event | category | flops | bytes accessed | tf_op | source)
XLA Modules:
  0.0 403.1 jit_solution(16055592062050895457)
XLA Ops:
  10.9 38.8 %all-gather.4.cloned.1.call-done = bf16[768,1816]{1,0:T(8,128)(2,1)} async-done(((bf16[96,1816]{1,0:T(8,128)(2,1)}), bf16[768,1816]{1,0:T(8,128)(2,1)}) %all-gather.4.cloned.1.call-update) | async-done | bytes 2789392 | tf_op jit(solution)/shard_map/all_gather | solution.py:138
  68.8 4.4 %fusion.119 = f32[4,128,1536]{2,1,0:T(8,128)} fusion(f32[24,1536,1]{1,0,2:T(8,128)S(1)} %reshape.302, f32[4,24,128]{2,1,0:T(8,128)S(1)} %fusion.109), kind=kOutput, calls=%fused_computation.223 | convolution fusion | flops 226492416 | bytes 3342336 | tf_op jit(solution)/shard_map/jvp(...h,hk->...k)/dot_general | solution.py:49
  77.6 12.1 %fusion.159 = (bf16[512,1792]{0,1:T(8,128)(2,1)S(1)}, f32[512,1792]{0,1:T(8,128)S(1)}, f32[512,1792]{0,1:T(8,128)}) fusion(f32[512,1792]{0,1:T(8,128)} %slice_convert_fusion, f32[1792]{0:T(1024)S(1)} %get-tuple-element.45, f32[3,1792]{0,1:T(8,128)S(1)} %convert_element_type.219, f32[1792]{0:T(1024)S(1)} %get-tuple-element.46, ...), kind=kLoop, calls=%fused_computation.274 | loop fusion | flops 14680064 | bytes 12902400 | tf_op jit(solution)/shard_map/convert.8
  96.4 4.6 %multiply_convert_fusion.4 = (bf16[4,128,1536]{2,1,0:T(8,128)(2,1)S(1)}, f32[4,128,1536]{2,1,0:T(8,128)}) fusion(f32[4,128,1536]{2,1,0:T(8,128)S(1)} %bitcast.277, f32[24,1536,1]{1,0,2:T(8,128)S(1)} %reshape.302, f32[3,4,8,128]{3,2,1,0:T(8,128)S(1)} %get-tuple-element.72, f32[4,24]{1,0:T(4,128)S(1)} %slice_reduce_fusion.1, f32[4,24,128]{2,1,0:T(8,128)S(1)} %fusion.109), kind=kOutput, calls=%fused_computation.76 | convolution fusion | flops 228089856 | bytes 8110464 | tf_op jit(solution)/shard_map/jvp(...h,hk->...k)/dot_general | solution.py:49
  116.5 5.3 %fusion.28 = f32[4,24,128,64]{2,3,1,0:T(8,128)} fusion(f32[4,24,128]{2,1,0:T(8,128)} %copy.85, f32[4,128,128]{2,1,0:T(8,128)S(1)} %fusion.88, f32[4,24,128]{2,1,0:T(8,128)S(1)} %fusion.109, pred[128,128]{1,0:T(8,128)(4,1)} %iota_compare_fusion, bf16[4,128,24,64]{1,0,3,2:T(4,128)(2,1)} %convert_element_type.225), kind=kOutput, calls=%fused_computation.81 | convolution fusion | flops 210763776 | bytes 5095424 | tf_op jit(solution)/shard_map/jvp(chts,chsp->chtp)/dot_general | solution.py:30
  141.3 5.8 %multiply_reduce_fusion.9 = (f32[512]{0:T(512)S(1)}, bf16[512,1536]{0,1:T(8,128)(2,1)}) fusion(bf16[512,1536]{0,1:T(8,128)(2,1)} %add_convert_fusion.1, bf16[768,1536]{1,0:T(8,128)(2,1)} %all-gather.6.cloned.1.call-done, bf16[1,512,768]{2,1,0:T(8,128)(2,1)} %param.11, f32[768]{0:T(1024)} %param.12, f32[512]{0:T(512)S(1)} %get-tuple-element.87), kind=kOutput, calls=%fused_computation.73 | convolution fusion | flops 1217396224 | bytes 6298624 | tf_op jit(solution)/shard_map/dot_general | solution.py:122
  147.7 6.3 %fusion.22 = (f32[1536]{0:T(1024)}, f32[512]{0:T(512)S(1)}, bf16[1536,512]{1,0:T(8,128)(2,1)S(1)}) fusion(f32[512]{0:T(512)} %get-tuple-element.89, bf16[512,1536]{0,1:T(8,128)(2,1)} %get-tuple-element.95, bf16[512,1536]{0,1:T(8,128)(2,1)} %add_convert_fusion.1, f32[1536]{0:T(1024)} %param.19, bf16[1536,768]{1,0:T(8,128)(2,1)} %all-gather.8.cloned.1.call-done, ...), kind=kOutput, calls=%fused_computation.59 | convolution fusion | flops 1219753984 | bytes 7880704 | tf_op jit(solution)/shard_map/dot_general | solution.py:126
  164.6 5.2 %fusion.27 = f32[4,24,128,64]{2,3,1,0:T(8,128)} fusion(f32[4,24,128]{2,1,0:T(8,128)} %copy.85, f32[4,128,128]{2,1,0:T(8,128)} %copy-done.45, f32[4,24,128]{2,1,0:T(8,128)S(1)} %fusion.109, pred[128,128]{1,0:T(8,128)(4,1)} %iota_compare_fusion, bf16[4,128,24,64]{1,0,3,2:T(4,128)(2,1)} %convert_element_type.247), kind=kOutput, calls=%fused_computation.80 | convolution fusion | flops 210763776 | bytes 5095424 | tf_op jit(solution)/shard_map/transpose(jvp(chts,chtp->chsp))/dot_general | solution.py:95
  173.8 4.7 %convolution_convert_fusion.2 = bf16[768,1536]{1,0:T(8,128)(2,1)} fusion(bf16[512,1536]{0,1:T(8,128)(2,1)} %get-tuple-element.65, bf16[1,512,768]{2,1,0:T(8,128)(2,1)} %param.11, f32[768]{0:T(1024)} %param.12, f32[512]{0:T(512)S(1)} %get-tuple-element.87), kind=kOutput, calls=%fused_computation.40 | convolution fusion | flops 1210712064 | bytes 4723712 | tf_op jit(solution)/shard_map/dot_general | solution.py:132
  178.6 8.4 %fusion.9 = (f32[4,24,128]{2,1,0:T(8,128)}, f32[4,24,128]{2,1,0:T(8,128)}, f32[4,24,128]{2,1,0:T(8,128)}, bf16[4,128,128]{2,1,0:T(8,128)(2,1)S(1)}) fusion(f32[4,24,128]{2,1,0:T(8,128)} %copy.85, f32[4,128,128]{2,1,0:T(8,128)} %copy-done.45, f32[4,24,128]{2,1,0:T(8,128)S(1)} %fusion.109, pred[128,128]{1,0:T(8,128)(4,1)} %iota_compare_fusion, ...), kind=kOutput, calls=%fused_computation.42 | convolution fusion | flops 224817152 | bytes 3801088 | tf_op jit(solution)/shard_map/transpose(jvp(chtp,chsp->chts))/dot_general | solution.py:95
  192.8 5.0 %multiply_reduce_fusion.7 = (f32[4,1536]{1,0:T(4,128)S(1)}, f32[128,1536]{1,0:T(8,128)}, f32[4,128,1536]{2,1,0:T(8,128)}) fusion(f32[128,1536]{1,0:T(8,128)} %copy-done.19, f32[4,1536]{1,0:T(4,128)} %fusion.165, bf16[4,128,1536]{2,1,0:T(8,128)(2,1)} %copy-done.25, bf16[16,4,8,128]{3,2,1,0:T(8,128)(2,1)} %get-tuple-element.74), kind=kOutput, calls=%fused_computation.61 | convolution fusion | flops 204269568 | bytes 6471680 | tf_op jit(solution)/shard_map/transpose(jvp(ctn,ctk->cnk))/dot_general | solution.py:97
  208.6 5.8 %convolution_convert_fusion = bf16[1536,768]{1,0:T(8,128)(2,1)} fusion(bf16[1,512,768]{2,1,0:T(8,128)(2,1)} %param.21, f32[1536]{0:T(1024)} %param.19, f32[512]{0:T(512)} %get-tuple-element.89, bf16[512,1536]{0,1:T(8,128)(2,1)} %add_convert_fusion.1, bf16[512,1536]{0,1:T(8,128)(2,1)} %get-tuple-element.95), kind=kOutput, calls=%fused_computation.38 | convolution fusion | flops 1217003520 | bytes 6299648 | tf_op jit(solution)/shard_map/dot_general | solution.py:132
  223.3 4.4 %collective-permute-done.7 = bf16[128,1536]{1,0:T(8,128)(2,1)} collective-permute-done((bf16[128,1536]{1,0:T(8,128)(2,1)}, bf16[128,1536]{1,0:T(8,128)(2,1)}, u32[]{:S(2)}, u32[]{:S(2)}) %collective-permute-start.7) | collective-permute-done | bytes 393248 | tf_op jit(solution)/shard_map/transpose(jvp())/ppermute | solution.py:54
  245.7 4.6 %multiply_reduce_fusion.6 = (f32[1536]{0:T(1024)}, f32[512,1536]{0,1:T(8,128)S(1)}) fusion(bf16[512,1536]{0,1:T(8,128)(2,1)S(1)} %copy-done.10, f32[512,1792]{0,1:T(8,128)} %copy-done.2, f32[512,1536]{0,1:T(8,128)} %copy.117, f32[1536]{0:T(1024)S(1)} %copy-done.62), kind=kLoop, calls=%fused_computation.60 | loop fusion | flops 3930624 | bytes 11022336 | tf_op jit(solution)/shard_map/transpose(jvp())/reduce_sum | solution.py:118
  251.1 9.7 %multiply_reduce_fusion.4 = (f32[1792]{0:T(1024)}, f32[1792]{0:T(1024)}, f32[1792]{0:T(1024)}, f32[1792]{0:T(1024)S(1)}, f32[1792]{0:T(1024)}, /*index=5*/f32[512,1792]{0,1:T(8,128)S(1)}) fusion(f32[512,1792]{0,1:T(8,128)S(1)} %copy-done.3, f32[3,1792]{0,1:T(8,128)S(1)} %copy-done.18, bf16[512,1816]{0,1:T(8,128)(2,1)} %copy-done.16, ...), kind=kLoop, calls=%fused_computation.27 | loop fusion | flops 22011136 | bytes 16572416 | tf_op jit(solution)/shard_map/transpose(jvp())/reduce_sum | solution.py:107
  260.8 4.7 %broadcast_multiply_fusion = (f32[512,1792]{0,1:T(8,128)S(1)}, f32[512,1792]{0,1:T(8,128)}, f32[512,1792]{0,1:T(8,128)}, f32[512,1792]{0,1:T(8,128)}) fusion(f32[512,1792]{0,1:T(8,128)S(1)} %get-tuple-element.53, f32[1792]{0:T(1024)S(1)} %copy-done.59, f32[1792]{0:T(1024)S(1)} %copy-done.55, f32[1792]{0:T(1024)S(1)} %copy-done.57, f32[1792]{0:T(1024)S(1)} %copy-done.61), kind=kLoop, calls=%fused_computation.84 | loop fusion | flops 3670016 | bytes 18378752 | tf_op jit(solution)/shard_map/transpose(jvp())/mul | solution.py:107
  265.5 8.2 %pad_add_fusion = f32[515,1792]{0,1:T(8,128)S(1)} fusion(f32[512,1792]{0,1:T(8,128)} %get-tuple-element.67, f32[512,1792]{0,1:T(8,128)} %get-tuple-element.68, f32[512,1792]{0,1:T(8,128)} %get-tuple-element.69, f32[512,1792]{0,1:T(8,128)S(1)} %get-tuple-element.66), kind=kLoop, calls=%fused_computation.15 | loop fusion | flops 2768640 | bytes 18371584 | tf_op jit(solution)/shard_map/transpose(jvp())/add_any | solution.py:107
  275.3 4.9 %fusion.63 = f32[4,24,128]{2,1,0:T(8,128)S(1)} fusion(f32[24,1536,1]{1,0,2:T(8,128)S(1)} %reshape.302, f32[4,128,1536]{2,1,0:T(8,128)} %get-tuple-element.93, f32[4,128,1536]{2,1,0:T(8,128)S(1)} %bitcast.280, f32[4,1,24]{1,2,0:T(8,128)S(1)} %copy-done.49, f32[4,24,128]{2,1,0:T(8,128)S(1)} %copy-done.64, f32[4,24,128]{2,1,0:T(8,128)S(1)} %copy-done.63, ...), kind=kOutput, calls=%fused_computation.122 | convolution fusion | flops 227401728 | bytes 6734592 | tf_op jit(solution)/shard_map/transpose(jvp(...h,hk->...k))/dot_general | solution.py:49
  281.6 4.9 %collective-permute-done.9 = bf16[3,1792]{0,1:T(8,128)(2,1)S(1)} collective-permute-done((bf16[3,1792]{0,1:T(8,128)(2,1)S(1)}, bf16[3,1792]{0,1:T(8,128)(2,1)S(1)}, u32[]{:S(2)}, u32[]{:S(2)}) %collective-permute-start.9) | collective-permute-done | bytes 10784 | tf_op jit(solution)/shard_map/transpose(jvp())/ppermute | solution.py:54
  291.1 4.9 %fusion.166 = f32[512,768]{1,0:T(8,128)} fusion(bf16[512,1536]{0,1:T(8,128)(2,1)} %get-tuple-element.65, bf16[768,1536]{1,0:T(8,128)(2,1)} %all-gather.6.cloned.1.call-done), kind=kOutput, calls=%fused_computation.278 | convolution fusion | flops 1207959552 | bytes 5505024 | tf_op jit(solution)/shard_map/dot_general | solution.py:126
  299.4 5.5 %fusion.40 = (f32[768]{0:T(1024)S(1)}, f32[512]{0:T(512)S(1)}, f32[512,768]{1,0:T(8,128)}) fusion(bf16[1,512,768]{2,1,0:T(8,128)(2,1)S(1)} %copy-done.37, f32[512]{0:T(512)S(1)} %copy-done.80, f32[768]{0:T(1024)S(1)} %copy-done.87, f32[512,768]{1,0:T(8,128)} %fusion.166, bf16[768,1816]{1,0:T(8,128)(2,1)} %all-gather.4.cloned.1.call-done, ...), kind=kOutput, calls=%fused_computation.99 | convolution fusion | flops 1435024128 | bytes 8591360 | tf_op jit(solution)/shard_map/dot_general | solution.py:126
  305.0 40.2 %psum.7 = f32[11336]{0:T(1024)S(1)} all-reduce(f32[11336]{0:T(1024)S(1)} %concatenate.15), channel_id=1, replica_groups=mesh['seq'=4,'fsdp'=8] {'seq','fsdp'}, use_global_device_ids=true, to_apply=%region_30.31 | all-reduce | flops 11336 | bytes 90688 | tf_op jit(solution)/shard_map/psum | solution.py:228
  358.8 11.4 %collective-permute-done.20 = bf16[192,768]{1,0:T(8,128)(2,1)S(1)} collective-permute-done((bf16[192,768]{1,0:T(8,128)(2,1)}, bf16[192,768]{1,0:T(8,128)(2,1)S(1)}, u32[]{:S(2)}, u32[]{:S(2)}) %collective-permute-start.20) | collective-permute-done | bytes 294944 | tf_op jit(solution)/shard_map/ppermute | solution.py:145
  381.8 8.4 %collective-permute-done.17 = bf16[96,1816]{1,0:T(8,128)(2,1)S(1)} collective-permute-done((bf16[96,1816]{1,0:T(8,128)(2,1)}, bf16[96,1816]{1,0:T(8,128)(2,1)S(1)}, u32[]{:S(2)}, u32[]{:S(2)}) %collective-permute-start.17) | collective-permute-done | bytes 348704 | tf_op jit(solution)/shard_map/ppermute | solution.py:145
  (357 shorter events, 169.2 us)
Async XLA Ops:
  7.2 42.5 %all-gather.4.cloned.1.call-start = ((), (), s32[]{:S(2)}) async-start(), calls=%async_computation.3 | async-start | bytes 3317760 | tf_op jit(solution)/shard_map/all_gather | solution.py:138
  9.1 132.1 %all-gather.6.cloned.1.call-start = ((), (), s32[]{:S(2)}) async-start(), calls=%async_computation.4 | async-start | bytes 2654208 | tf_op jit(solution)/shard_map/all_gather | solution.py:138
  49.7 97.9 %all-gather.8.cloned.1.call-start = ((), (), s32[]{:S(2)}) async-start(), calls=%async_computation.5 | async-start | bytes 2654208 | tf_op jit(solution)/shard_map/all_gather | solution.py:138
  57.6 18.2 %collective-permute-start.4 = (f32[24]{0:T(128)S(1)}, f32[24]{0:T(128)S(1)}, u32[]{:S(2)}, u32[]{:S(2)}) collective-permute-start(f32[24]{0:T(128)S(1)} %get-tuple-element.41), channel_id=1, source_target_pairs={{0,16},{8,24},{1,17},{9,25},{2,18},{10,26},{3,19},{11,27},{4,20},{... | collective-permute-start | bytes 296 | tf_op jit(solution)/shard_map/jvp()/ppermute | solution.py:54
  61.0 14.8 %collective-permute-start.2 = (f32[24]{0:T(128)S(1)}, f32[24]{0:T(128)S(1)}, u32[]{:S(2)}, u32[]{:S(2)}) collective-permute-start(f32[24]{0:T(128)S(1)} %get-tuple-element.41), channel_id=1, source_target_pairs={{0,8},{8,16},{16,24},{1,9},{9,17},{17,25},{2,10},{10,18},{18,26},{... | collective-permute-start | bytes 296 | tf_op jit(solution)/shard_map/jvp()/ppermute | solution.py:54
  75.6 272.7 %reduce-scatter.4.cloned.1.call-start = ((), (), s32[]{:S(2)}) async-start(), calls=%async_computation.6 | async-start | bytes 2654208 | tf_op jit(solution)/shard_map/reduce_scatter | solution.py:152
  103.2 23.5 %collective-permute-start.5 = (bf16[128,1536]{1,0:T(8,128)(2,1)}, bf16[128,1536]{1,0:T(8,128)(2,1)}, u32[]{:S(2)}, u32[]{:S(2)}) collective-permute-start(bf16[128,1536]{1,0:T(8,128)(2,1)} %get-tuple-element.56), channel_id=1, source_target_pairs={{0,24},{1,25},{2,26},{3,27},{4,28},{5,29},{6,30},{7,31}} | collective-permute-start | bytes 1179656 | tf_op jit(solution)/shard_map/jvp()/ppermute | solution.py:54
  107.0 19.7 %collective-permute-start.3 = (bf16[128,1536]{1,0:T(8,128)(2,1)}, bf16[128,1536]{1,0:T(8,128)(2,1)}, u32[]{:S(2)}, u32[]{:S(2)}) collective-permute-start(bf16[128,1536]{1,0:T(8,128)(2,1)} %get-tuple-element.56), channel_id=1, source_target_pairs={{0,16},{8,24},{1,17},{9,25},{2,18},{10,26},{3,19},{11,27},{4,20},{... | collective-permute-start | bytes 1179656 | tf_op jit(solution)/shard_map/jvp()/ppermute | solution.py:54
  109.5 17.2 %collective-permute-start.1 = (bf16[128,1536]{1,0:T(8,128)(2,1)}, bf16[128,1536]{1,0:T(8,128)(2,1)}, u32[]{:S(2)}, u32[]{:S(2)}) collective-permute-start(bf16[128,1536]{1,0:T(8,128)(2,1)} %get-tuple-element.56), channel_id=1, source_target_pairs={{0,8},{8,16},{16,24},{1,9},{9,17},{17,25},{2,10},{10,18},{18,26},{... | collective-permute-start | bytes 1179656 | tf_op jit(solution)/shard_map/jvp()/ppermute | solution.py:54
  178.5 174.1 %reduce-scatter.8.cloned.1.call-start = ((), (), s32[]{:S(2)}) async-start(), calls=%async_computation.8 | async-start | bytes 2654208 | tf_op jit(solution)/shard_map/reduce_scatter | solution.py:152
  203.4 18.7 %collective-permute-start.10 = (f32[24]{0:T(128)}, f32[24]{0:T(128)}, u32[]{:S(2)}, u32[]{:S(2)}) collective-permute-start(f32[24]{0:T(128)} %fusion.66), channel_id=1, source_target_pairs={{16,0},{24,8},{17,1},{25,9},{18,2},{26,10},{19,3},{27,11},{20,4},{... | collective-permute-start | bytes 296 | tf_op jit(solution)/shard_map/transpose(jvp())/ppermute | solution.py:54
  204.7 18.6 %collective-permute-start.8 = (bf16[128,1536]{1,0:T(8,128)(2,1)}, bf16[128,1536]{1,0:T(8,128)(2,1)}, u32[]{:S(2)}, u32[]{:S(2)}) collective-permute-start(bf16[128,1536]{1,0:T(8,128)(2,1)} %get-tuple-element.78), channel_id=1, source_target_pairs={{8,0},{16,8},{24,16},{9,1},{17,9},{25,17},{10,2},{18,10},{26,18},{... | collective-permute-start | bytes 1179656 | tf_op jit(solution)/shard_map/transpose(jvp())/ppermute | solution.py:54
  206.0 21.7 %collective-permute-start.7 = (bf16[128,1536]{1,0:T(8,128)(2,1)}, bf16[128,1536]{1,0:T(8,128)(2,1)}, u32[]{:S(2)}, u32[]{:S(2)}) collective-permute-start(bf16[128,1536]{1,0:T(8,128)(2,1)} %get-tuple-element.79), channel_id=1, source_target_pairs={{16,0},{24,8},{17,1},{25,9},{18,2},{26,10},{19,3},{27,11},{20,4},{... | collective-permute-start | bytes 1179656 | tf_op jit(solution)/shard_map/transpose(jvp())/ppermute | solution.py:54
  207.3 20.4 %collective-permute-start.6 = (bf16[128,1536]{1,0:T(8,128)(2,1)}, bf16[128,1536]{1,0:T(8,128)(2,1)}, u32[]{:S(2)}, u32[]{:S(2)}) collective-permute-start(bf16[128,1536]{1,0:T(8,128)(2,1)} %get-tuple-element.80), channel_id=1, source_target_pairs={{24,0},{25,1},{26,2},{27,3},{28,4},{29,5},{30,6},{31,7}} | collective-permute-start | bytes 1179656 | tf_op jit(solution)/shard_map/transpose(jvp())/ppermute | solution.py:54
  219.1 153.9 %reduce-scatter.6.cloned.1.call-start = ((), (), s32[]{:S(2)}) async-start(), calls=%async_computation.7 | async-start | bytes 3317760 | tf_op jit(solution)/shard_map/reduce_scatter | solution.py:152
  273.7 12.7 %collective-permute-start.9 = (bf16[3,1792]{0,1:T(8,128)(2,1)S(1)}, bf16[3,1792]{0,1:T(8,128)(2,1)S(1)}, u32[]{:S(2)}, u32[]{:S(2)}) collective-permute-start(bf16[3,1792]{0,1:T(8,128)(2,1)S(1)} %split.15), channel_id=1, source_target_pairs={{8,0},{16,8},{24,16},{9,1},{17,9},{25,17},{10,2},{18,10},{26,18},{... | collective-permute-start | bytes 32264 | tf_op jit(solution)/shard_map/transpose(jvp())/ppermute | solution.py:54
  348.3 24.7 %collective-permute-start.14 = (bf16[96,1536]{1,0:T(8,128)(2,1)}, bf16[96,1536]{1,0:T(8,128)(2,1)S(1)}, u32[]{:S(2)}, u32[]{:S(2)}) collective-permute-start(bf16[96,1536]{1,0:T(8,128)(2,1)} %reduce-scatter.4.cloned.1.call-done), channel_id=1, source_target_pairs={{0,24},{8,16},{16,8},{24,0},{1,25},{9,17},{17,9},{25,1},{2,26},{10... | collective-permute-start | bytes 884744 | tf_op jit(solution)/shard_map/ppermute | solution.py:145
  352.0 22.4 %collective-permute-start.13 = (bf16[96,1536]{1,0:T(8,128)(2,1)}, bf16[96,1536]{1,0:T(8,128)(2,1)S(1)}, u32[]{:S(2)}, u32[]{:S(2)}) collective-permute-start(bf16[96,1536]{1,0:T(8,128)(2,1)} %reduce-scatter.4.cloned.1.call-done), channel_id=1, source_target_pairs={{0,16},{8,24},{16,0},{24,8},{1,17},{9,25},{17,1},{25,9},{2,18},{10... | collective-permute-start | bytes 884744 | tf_op jit(solution)/shard_map/ppermute | solution.py:145
  352.0 22.5 %collective-permute-start.12 = (bf16[96,1536]{1,0:T(8,128)(2,1)}, bf16[96,1536]{1,0:T(8,128)(2,1)S(1)}, u32[]{:S(2)}, u32[]{:S(2)}) collective-permute-start(bf16[96,1536]{1,0:T(8,128)(2,1)} %reduce-scatter.4.cloned.1.call-done), channel_id=1, source_target_pairs={{0,8},{8,0},{16,24},{24,16},{1,9},{9,1},{17,25},{25,17},{2,10},{10... | collective-permute-start | bytes 884744 | tf_op jit(solution)/shard_map/ppermute | solution.py:145
  352.6 17.6 %collective-permute-start.20 = (bf16[192,768]{1,0:T(8,128)(2,1)}, bf16[192,768]{1,0:T(8,128)(2,1)S(1)}, u32[]{:S(2)}, u32[]{:S(2)}) collective-permute-start(bf16[192,768]{1,0:T(8,128)(2,1)} %reduce-scatter.8.cloned.1.call-done), channel_id=1, source_target_pairs={{0,24},{8,16},{16,8},{24,0},{1,25},{9,17},{17,9},{25,1},{2,26},{10... | collective-permute-start | bytes 884744 | tf_op jit(solution)/shard_map/ppermute | solution.py:145
  358.8 18.6 %collective-permute-start.19 = (bf16[192,768]{1,0:T(8,128)(2,1)S(1)}, bf16[192,768]{1,0:T(8,128)(2,1)S(1)}, u32[]{:S(2)}, u32[]{:S(2)}) collective-permute-start(bf16[192,768]{1,0:T(8,128)(2,1)S(1)} %copy-done.44), channel_id=1, source_target_pairs={{0,16},{8,24},{16,0},{24,8},{1,17},{9,25},{17,1},{25,9},{2,18},{10... | collective-permute-start | bytes 884744 | tf_op jit(solution)/shard_map/ppermute | solution.py:145
  373.0 17.3 %collective-permute-start.17 = (bf16[96,1816]{1,0:T(8,128)(2,1)}, bf16[96,1816]{1,0:T(8,128)(2,1)S(1)}, u32[]{:S(2)}, u32[]{:S(2)}) collective-permute-start(bf16[96,1816]{1,0:T(8,128)(2,1)} %reduce-scatter.6.cloned.1.call-done), channel_id=1, source_target_pairs={{0,24},{8,16},{16,8},{24,0},{1,25},{9,17},{17,9},{25,1},{2,26},{10... | collective-permute-start | bytes 1046024 | tf_op jit(solution)/shard_map/ppermute | solution.py:145
  374.4 18.1 %collective-permute-start.16 = (bf16[96,1816]{1,0:T(8,128)(2,1)}, bf16[96,1816]{1,0:T(8,128)(2,1)S(1)}, u32[]{:S(2)}, u32[]{:S(2)}) collective-permute-start(bf16[96,1816]{1,0:T(8,128)(2,1)} %reduce-scatter.6.cloned.1.call-done), channel_id=1, source_target_pairs={{0,16},{8,24},{16,0},{24,8},{1,17},{9,25},{17,1},{25,9},{2,18},{10... | collective-permute-start | bytes 1046024 | tf_op jit(solution)/shard_map/ppermute | solution.py:145
  374.5 20.1 %collective-permute-start.15 = (bf16[96,1816]{1,0:T(8,128)(2,1)}, bf16[96,1816]{1,0:T(8,128)(2,1)S(1)}, u32[]{:S(2)}, u32[]{:S(2)}) collective-permute-start(bf16[96,1816]{1,0:T(8,128)(2,1)} %reduce-scatter.6.cloned.1.call-done), channel_id=1, source_target_pairs={{0,8},{8,0},{16,24},{24,16},{1,9},{9,1},{17,25},{25,17},{2,10},{10... | collective-permute-start | bytes 1046024 | tf_op jit(solution)/shard_map/ppermute | solution.py:145
  (102 other events, 1062.0 us)
Sparse Core Ops, SparseCore 0:
  10.3 39.3 all-gather.3
  51.3 30.4 all-gather.5
  83.5 30.7 all-gather.7
  178.6 33.2 reduce-scatter.3
  219.2 40.7 reduce-scatter.7
  291.1 38.4 reduce-scatter.5

commit v3 on v1

--- a/solution.py
+++ b/solution.py
@@ -141,6 +141,16 @@
 def reduced(part):
     rows = lax.psum_scatter(part.astype(bf16), "fsdp", scatter_dimension=0, tiled=True)
     return lax.psum(rows, "seq").astype(f32)
+
+
+def everywhere(values):
+    for axis in ("fsdp", "seq"):
+        count = lax.axis_size(axis)
+        other = 1
+        while other < count:
+            values = values + lax.ppermute(values, axis, [(at, at ^ other) for at in range(count)])
+            other *= 2
+    return values
 
 
 def body(
@@ -215,7 +225,7 @@
         skip_grad,
         gain_grad,
     )
-    flat = lax.psum(jnp.concatenate([each.reshape(-1) for each in small]), ("seq", "fsdp"))
+    flat = everywhere(jnp.concatenate([each.reshape(-1) for each in small]))
     sums, at = [], 0
     for each in small:
         sums.append(flat[at : at + each.size].reshape(each.shape))

time: 390 us -> 391 us (level)
  blocking collectives: 38.5 us -> 0 us
  waiting for transfers between devices: 84.2 us -> 114 us
  starting transfers between devices: 25.8 us -> 32.3 us
    psum x1 -> x0, blocking collectives: 38.5 us -> none  [body(): lax.psum(jnp.concatenate([each.reshape(-1) for each in small]), ('seq', '...]
    psum x1, waiting for transfers between devices: 7.04 us -> 42.5 us  [reduced(): return lax.psum(rows, 'seq').astype(f32)]
    reduce_scatter x3, waiting for transfers between devices: 31.5 us -> 12.1 us  [reduced(): lax.psum_scatter(part.astype(bf16), 'fsdp', scatter_dimension=0, tiled=True)]
    ppermute x0 -> x5, waiting for transfers between devices: none -> 14.1 us  [everywhere(): lax.ppermute(values, axis, [(at, at ^ other) for at in range(count)])]
    ppermute x0 -> x5, starting transfers between devices: none -> 6.23 us  [everywhere(): lax.ppermute(values, axis, [(at, at ^ other) for at in range(count)])]
  transfers between devices with their start and end apart: 19 -> 24, of which waited for: 5 -> 9; matrix products, arithmetic and copies ran while one was open for 49% -> 50% of each run, Pallas kernels for 0% -> 0%
where the time goes in v3:
time: 391 us; the launch traced here: 385 us
  waiting for transfers between devices  114 us (29%)
  matrix products  96.2 us (25%)
  other arithmetic  76.4 us (20%)
  local copies, waits for them, and re-layouts  50.1 us (13%)
  starting transfers between devices  32.3 us (8%)
  between operations  15.8 us (4%)
    psum x1, waiting for transfers between devices, reduced(): return lax.psum(rows, 'seq').astype(f32)  42.5 us
    all_gather x3, waiting for transfers between devices, gathered(): return lax.all_gather(rows, 'fsdp', axis=0, tiled=True)  38.8 us
    ppermute x12, starting transfers between devices, shifted(): lax.ppermute(values, 'seq', [(at, at + by) for at in range(count - by)])  24.8 us
    dot_general x14, matrix products, over_heads(): return jnp.einsum('...h,hk->...k', values, spread, precision=precise)  23 us
    dot_general x3, matrix products, times_transposed(): lax.dot_general(left_mat, right_mat, (((1,), (1,)), ((), ())), preferred_...  17.5 us
    ppermute x5, waiting for transfers between devices, everywhere(): lax.ppermute(values, axis, [(at, at ^ other) for at in range(count)])  14.1 us
    dot_general x3, matrix products, plain(): return jnp.dot(left_mat, right_mat, preferred_element_type=f32)  13.6 us
    another operation x2, other arithmetic  12.8 us
  transfers between devices with their start and end apart: 24, of which 9 were waited for; matrix products, arithmetic and copies ran while one was open for 50% of the time, Pallas kernels for 0%

profile of v3, /device:TPU:0, one launch (start us, length us, event | category | flops | bytes accessed | tf_op | source)
XLA Modules:
  0.0 385.2 jit_solution(14573703514975189556)
XLA Ops:
  10.9 38.8 %all-gather.4.cloned.1.call-done = bf16[768,1816]{1,0:T(8,128)(2,1)} async-done(((bf16[96,1816]{1,0:T(8,128)(2,1)}), bf16[768,1816]{1,0:T(8,128)(2,1)}) %all-gather.4.cloned.1.call-update) | async-done | bytes 2789392 | tf_op jit(solution)/shard_map/all_gather | solution.py:138
  68.8 4.4 %fusion.119 = f32[4,128,1536]{2,1,0:T(8,128)} fusion(f32[24,1536,1]{1,0,2:T(8,128)S(1)} %reshape.302, f32[4,24,128]{2,1,0:T(8,128)S(1)} %fusion.109), kind=kOutput, calls=%fused_computation.220 | convolution fusion | flops 226492416 | bytes 3342336 | tf_op jit(solution)/shard_map/jvp(...h,hk->...k)/dot_general | solution.py:49
  77.9 12.0 %fusion.159 = (bf16[512,1792]{0,1:T(8,128)(2,1)S(1)}, f32[512,1792]{0,1:T(8,128)S(1)}, f32[512,1792]{0,1:T(8,128)}) fusion(f32[512,1792]{0,1:T(8,128)} %slice_convert_fusion, f32[1792]{0:T(1024)S(1)} %get-tuple-element.45, f32[3,1792]{0,1:T(8,128)S(1)} %convert_element_type.188, f32[1792]{0:T(1024)S(1)} %get-tuple-element.46, ...), kind=kLoop, calls=%fused_computation.271 | loop fusion | flops 14680064 | bytes 12902400 | tf_op jit(solution)/shard_map/convert.9
  96.6 4.6 %multiply_convert_fusion.4 = (bf16[4,128,1536]{2,1,0:T(8,128)(2,1)S(1)}, f32[4,128,1536]{2,1,0:T(8,128)}) fusion(f32[4,128,1536]{2,1,0:T(8,128)S(1)} %bitcast.277, f32[24,1536,1]{1,0,2:T(8,128)S(1)} %reshape.302, f32[3,4,8,128]{3,2,1,0:T(8,128)S(1)} %get-tuple-element.75, f32[4,24]{1,0:T(4,128)S(1)} %slice_reduce_fusion.1, f32[4,24,128]{2,1,0:T(8,128)S(1)} %fusion.109), kind=kOutput, calls=%fused_computation.76 | convolution fusion | flops 228089856 | bytes 8110464 | tf_op jit(solution)/shard_map/jvp(...h,hk->...k)/dot_general | solution.py:49
  116.0 5.3 %fusion.28 = f32[4,24,128,64]{2,3,1,0:T(8,128)} fusion(f32[4,24,128]{2,1,0:T(8,128)} %copy.85, f32[4,128,128]{2,1,0:T(8,128)} %fusion.88, f32[4,24,128]{2,1,0:T(8,128)S(1)} %fusion.109, pred[128,128]{1,0:T(8,128)(4,1)} %iota_compare_fusion, bf16[4,128,24,64]{1,0,3,2:T(4,128)(2,1)} %convert_element_type.194), kind=kOutput, calls=%fused_computation.81 | convolution fusion | flops 210763776 | bytes 5095424 | tf_op jit(solution)/shard_map/jvp(chts,chsp->chtp)/dot_general | solution.py:30
  136.4 4.3 %add_convert_fusion.1 = bf16[512,1536]{0,1:T(8,128)(2,1)} fusion(f32[512,1536]{0,1:T(8,128)} %copy.114, f32[1536]{0:T(1024)} %convolution_reduce_fusion, f32[512,1792]{0,1:T(8,128)} %copy-done.2), kind=kLoop, calls=%fused_computation.74 | loop fusion | flops 2359296 | bytes 7870464 | tf_op jit(solution)/shard_map/convert_element_type | solution.py:190
  140.8 4.8 %multiply_reduce_fusion.9 = (f32[512]{0:T(512)S(1)}, bf16[512,1536]{0,1:T(8,128)(2,1)S(1)}) fusion(bf16[512,1536]{0,1:T(8,128)(2,1)} %add_convert_fusion.1, bf16[768,1536]{1,0:T(8,128)(2,1)} %all-gather.6.cloned.1.call-done, bf16[1,512,768]{2,1,0:T(8,128)(2,1)} %param.11, f32[768]{0:T(1024)} %param.12, f32[512]{0:T(512)} %copy-done.83), kind=kOutput, calls=%fused_computation.73 | convolution fusion | flops 1217396224 | bytes 6298624 | tf_op jit(solution)/shard_map/dot_general | solution.py:122
  150.4 6.3 %fusion.22 = (f32[1536]{0:T(1024)}, f32[512]{0:T(512)S(1)}, bf16[1536,512]{1,0:T(8,128)(2,1)S(1)}) fusion(f32[512]{0:T(512)} %copy-done.85, bf16[512,1536]{0,1:T(8,128)(2,1)} %copy-done.41, bf16[512,1536]{0,1:T(8,128)(2,1)} %add_convert_fusion.1, f32[1536]{0:T(1024)} %param.19, bf16[1536,768]{1,0:T(8,128)(2,1)} %all-gather.8.cloned.1.call-done, ...), kind=kOutput, calls=%fused_computation.59 | convolution fusion | flops 1219753984 | bytes 7880704 | tf_op jit(solution)/shard_map/dot_general | solution.py:126
  182.4 7.3 %fusion.9 = (f32[4,24,128]{2,1,0:T(8,128)}, f32[4,24,128]{2,1,0:T(8,128)}, f32[4,24,128]{2,1,0:T(8,128)}, bf16[4,128,128]{2,1,0:T(8,128)(2,1)S(1)}) fusion(f32[4,24,128]{2,1,0:T(8,128)S(1)} %copy-done.70, f32[4,128,128]{2,1,0:T(8,128)S(1)} %copy-done.47, f32[4,24,128]{2,1,0:T(8,128)S(1)} %fusion.109, pred[128,128]{1,0:T(8,128)(4,1)S(1)} %copy-done.75, ...), kind=kOutput, calls=%fused_computation.42 | convolution fusion | flops 224817152 | bytes 3801088 | tf_op jit(solution)/shard_map/transpose(jvp(chtp,chsp->chts))/dot_general | solution.py:95
  205.0 4.7 %convolution_convert_fusion.2 = bf16[768,1536]{1,0:T(8,128)(2,1)} fusion(bf16[512,1536]{0,1:T(8,128)(2,1)} %get-tuple-element.68, bf16[1,512,768]{2,1,0:T(8,128)(2,1)} %param.11, f32[768]{0:T(1024)} %param.12, f32[512]{0:T(512)} %copy-done.83), kind=kOutput, calls=%fused_computation.40 | convolution fusion | flops 1210712064 | bytes 4723712 | tf_op jit(solution)/shard_map/dot_general | solution.py:132
  224.2 4.0 %copy.117 = f32[512,1536]{0,1:T(8,128)} copy(f32[512,1536]{1,0:T(8,128)} %bitcast.282) | data formatting | bytes 6291456 | tf_op jit(solution)/shard_map/transpose(jvp())/reshape | solution.py:71
  229.5 4.6 %multiply_reduce_fusion.6 = (f32[1536]{0:T(1024)}, f32[512,1536]{0,1:T(8,128)S(1)}) fusion(bf16[512,1536]{0,1:T(8,128)(2,1)S(1)} %copy-done.8, f32[512,1792]{0,1:T(8,128)} %copy-done.2, f32[512,1536]{0,1:T(8,128)} %copy.117, f32[1536]{0:T(1024)S(1)} %copy-done.66), kind=kLoop, calls=%fused_computation.60 | loop fusion | flops 3930624 | bytes 11022336 | tf_op jit(solution)/shard_map/transpose(jvp())/reduce_sum | solution.py:118
  234.8 9.1 %multiply_reduce_fusion.4 = (f32[1792]{0:T(1024)S(1)}, f32[1792]{0:T(1024)S(1)}, f32[1792]{0:T(1024)S(1)}, f32[1792]{0:T(1024)S(1)}, f32[1792]{0:T(1024)S(1)}, /*index=5*/f32[512,1792]{0,1:T(8,128)S(1)}) fusion(f32[512,1792]{0,1:T(8,128)S(1)} %copy-done.3, f32[3,1792]{0,1:T(8,128)S(1)} %copy-done.16, bf16[512,1816]{0,1:T(8,128)(2,1)} %copy-done.14, ...), kind=kLoop, calls=%fused_computation.27 | loop fusion | flops 22011136 | bytes 16572416 | tf_op jit(solution)/shard_map/transpose(jvp())/reduce_sum | solution.py:107
  243.9 4.7 %broadcast_multiply_fusion = (f32[512,1792]{0,1:T(8,128)S(1)}, f32[512,1792]{0,1:T(8,128)}, f32[512,1792]{0,1:T(8,128)}, f32[512,1792]{0,1:T(8,128)}) fusion(f32[512,1792]{0,1:T(8,128)S(1)} %get-tuple-element.56, f32[1792]{0:T(1024)S(1)} %copy-done.61, f32[1792]{0:T(1024)S(1)} %copy-done.57, f32[1792]{0:T(1024)S(1)} %copy-done.59, f32[1792]{0:T(1024)S(1)} %copy-done.63), kind=kLoop, calls=%fused_computation.84 | loop fusion | flops 3670016 | bytes 18378752 | tf_op jit(solution)/shard_map/transpose(jvp())/mul | solution.py:107
  248.6 8.3 %pad_add_fusion = f32[515,1792]{0,1:T(8,128)S(1)} fusion(f32[512,1792]{0,1:T(8,128)} %get-tuple-element.70, f32[512,1792]{0,1:T(8,128)} %get-tuple-element.71, f32[512,1792]{0,1:T(8,128)} %get-tuple-element.72, f32[512,1792]{0,1:T(8,128)S(1)} %get-tuple-element.69), kind=kLoop, calls=%fused_computation.15 | loop fusion | flops 2768640 | bytes 18371584 | tf_op jit(solution)/shard_map/transpose(jvp())/add_any | solution.py:107
  258.5 4.9 %fusion.63 = f32[4,24,128]{2,1,0:T(8,128)S(1)} fusion(f32[24,1536,1]{1,0,2:T(8,128)S(1)} %reshape.302, f32[4,128,1536]{2,1,0:T(8,128)} %get-tuple-element.96, f32[4,128,1536]{2,1,0:T(8,128)S(1)} %bitcast.280, f32[4,1,24]{1,2,0:T(8,128)S(1)} %copy-done.51, f32[4,24,128]{2,1,0:T(8,128)S(1)} %copy-done.68, f32[4,24,128]{2,1,0:T(8,128)S(1)} %copy-done.67, ...), kind=kOutput, calls=%fused_computation.121 | convolution fusion | flops 227401728 | bytes 6734592 | tf_op jit(solution)/shard_map/transpose(jvp(...h,hk->...k))/dot_general | solution.py:49
  264.8 6.4 %collective-permute-done.9 = bf16[3,1792]{0,1:T(8,128)(2,1)S(1)} collective-permute-done((bf16[3,1792]{0,1:T(8,128)(2,1)S(1)}, bf16[3,1792]{0,1:T(8,128)(2,1)S(1)}, u32[]{:S(2)}, u32[]{:S(2)}) %collective-permute-start.9) | collective-permute-done | bytes 10784 | tf_op jit(solution)/shard_map/transpose(jvp())/ppermute | solution.py:54
  277.4 4.7 %fusion.166 = f32[512,768]{1,0:T(8,128)} fusion(bf16[512,1536]{0,1:T(8,128)(2,1)} %get-tuple-element.68, bf16[768,1536]{1,0:T(8,128)(2,1)} %all-gather.6.cloned.1.call-done), kind=kOutput, calls=%fused_computation.275 | convolution fusion | flops 1207959552 | bytes 5505024 | tf_op jit(solution)/shard_map/dot_general | solution.py:126
  282.5 6.5 %fusion.40 = (f32[768]{0:T(1024)S(1)}, f32[512]{0:T(512)S(1)}, f32[512,768]{1,0:T(8,128)}) fusion(bf16[1,512,768]{2,1,0:T(8,128)(2,1)S(1)} %copy-done.37, f32[512]{0:T(512)S(1)} %copy-done.84, f32[768]{0:T(1024)S(1)} %copy-done.92, f32[512,768]{1,0:T(8,128)} %fusion.166, bf16[768,1816]{1,0:T(8,128)(2,1)} %all-gather.4.cloned.1.call-done, ...), kind=kOutput, calls=%fused_computation.99 | convolution fusion | flops 1435024128 | bytes 8591360 | tf_op jit(solution)/shard_map/dot_general | solution.py:126
  290.7 5.2 %collective-permute-done.13 = f32[11336]{0:T(1024)S(1)} collective-permute-done((f32[11336]{0:T(1024)S(1)}, f32[11336]{0:T(1024)S(1)}, u32[]{:S(2)}, u32[]{:S(2)}) %collective-permute-start.13) | collective-permute-done | bytes 45376 | tf_op jit(solution)/shard_map/ppermute | solution.py:151
  296.9 6.7 %collective-permute-done.14 = f32[11336]{0:T(1024)S(1)} collective-permute-done((f32[11336]{0:T(1024)S(1)}, f32[11336]{0:T(1024)S(1)}, u32[]{:S(2)}, u32[]{:S(2)}) %collective-permute-start.14) | collective-permute-done | bytes 45376 | tf_op jit(solution)/shard_map/ppermute | solution.py:151
  306.9 12.1 %reduce-scatter.6.cloned.1.call-done = bf16[96,1816]{1,0:T(8,128)(2,1)} async-done(((bf16[768,1816]{1,0:T(8,128)(2,1)}), bf16[96,1816]{1,0:T(8,128)(2,1)}) %reduce-scatter.6.cloned.1.call-update) | async-done | bytes 348688 | tf_op jit(solution)/shard_map/reduce_scatter | solution.py:142
  319.1 5.2 %fusion.50 = bf16[1,512,768]{2,1,0:T(8,128)(2,1)} fusion(bf16[1536,768]{1,0:T(8,128)(2,1)} %all-gather.8.cloned.1.call-done, bf16[1,512,768]{2,1,0:T(8,128)(2,1)S(1)} %copy-done.37, f32[1536]{0:T(1024)S(1)} %copy-done.79, f32[512]{0:T(512)S(1)} %copy-done.87, bf16[512,1536]{0,1:T(8,128)(2,1)S(1)} %copy-done.23, bf16[512,1536]{0,1:T(8,128)(2,1)} %copy-done.41), kind=kOutput, calls=%fused_computation.110 | convolution fusion | flops 1217003520 | bytes 7086080 | tf_op jit(solution)/shard_map/dot_general | solution.py:122
  331.6 42.5 %all-reduce.24.cloned.1.call-done = (bf16[96,1816]{1,0:T(8,128)(2,1)}, bf16[96,1536]{1,0:T(8,128)(2,1)}, bf16[192,768]{1,0:T(8,128)(2,1)}) async-done(((bf16[96,1816]{1,0:T(8,128)(2,1)}, bf16[96,1536]{1,0:T(8,128)(2,1)}, bf16[192,768]{1,0:T(8,128)(2,1)}), (bf16[96,1816]{1,0:T(8,128)(2,1)}, bf16[96,1536]{1,0:T(8,128)(2,1)}, bf16[192,768]{1,0:T(8,128)(2,1)})) %all-reduce.24.cloned.1.call-update) | async-done | bytes 938512 | tf_op jit(solution)/shard_map/psum | solution.py:143
  (364 shorter events, 151.9 us)
Async XLA Ops:
  7.2 42.5 %all-gather.4.cloned.1.call-start = ((), (), s32[]{:S(2)}) async-start(), calls=%async_computation.3 | async-start | bytes 3317760 | tf_op jit(solution)/shard_map/all_gather | solution.py:138
  9.1 131.6 %all-gather.6.cloned.1.call-start = ((), (), s32[]{:S(2)}) async-start(), calls=%async_computation.4 | async-start | bytes 2654208 | tf_op jit(solution)/shard_map/all_gather | solution.py:138
  49.7 100.7 %all-gather.8.cloned.1.call-start = ((), (), s32[]{:S(2)}) async-start(), calls=%async_computation.5 | async-start | bytes 2654208 | tf_op jit(solution)/shard_map/all_gather | solution.py:138
  57.6 18.5 %collective-permute-start.4 = (f32[24]{0:T(128)S(1)}, f32[24]{0:T(128)S(1)}, u32[]{:S(2)}, u32[]{:S(2)}) collective-permute-start(f32[24]{0:T(128)S(1)} %get-tuple-element.41), channel_id=1, source_target_pairs={{0,16},{8,24},{1,17},{9,25},{2,18},{10,26},{3,19},{11,27},{4,20},{... | collective-permute-start | bytes 296 | tf_op jit(solution)/shard_map/jvp()/ppermute | solution.py:54
  61.0 15.1 %collective-permute-start.2 = (f32[24]{0:T(128)S(1)}, f32[24]{0:T(128)S(1)}, u32[]{:S(2)}, u32[]{:S(2)}) collective-permute-start(f32[24]{0:T(128)S(1)} %get-tuple-element.41), channel_id=1, source_target_pairs={{0,8},{8,16},{16,24},{1,9},{9,17},{17,25},{2,10},{10,18},{18,26},{... | collective-permute-start | bytes 296 | tf_op jit(solution)/shard_map/jvp()/ppermute | solution.py:54
  65.2 12.6 %collective-permute-start = (bf16[3,1792]{0,1:T(8,128)(2,1)S(1)}, bf16[3,1792]{0,1:T(8,128)(2,1)S(1)}, u32[]{:S(2)}, u32[]{:S(2)}) collective-permute-start(bf16[3,1792]{0,1:T(8,128)(2,1)S(1)} %slice.129), channel_id=1, source_target_pairs={{0,8},{8,16},{16,24},{1,9},{9,17},{17,25},{2,10},{10,18},{18,26},{... | collective-permute-start | bytes 32264 | tf_op jit(solution)/shard_map/jvp()/ppermute | solution.py:54
  75.5 231.4 %reduce-scatter.8.cloned.1.call-start = ((), (), s32[]{:S(2)}) async-start(), calls=%async_computation.8 | async-start | bytes 2654208 | tf_op jit(solution)/shard_map/reduce_scatter | solution.py:142
  103.4 22.8 %collective-permute-start.5 = (bf16[128,1536]{1,0:T(8,128)(2,1)}, bf16[128,1536]{1,0:T(8,128)(2,1)}, u32[]{:S(2)}, u32[]{:S(2)}) collective-permute-start(bf16[128,1536]{1,0:T(8,128)(2,1)} %get-tuple-element.59), channel_id=1, source_target_pairs={{0,24},{1,25},{2,26},{3,27},{4,28},{5,29},{6,30},{7,31}} | collective-permute-start | bytes 1179656 | tf_op jit(solution)/shard_map/jvp()/ppermute | solution.py:54
  106.9 19.3 %collective-permute-start.3 = (bf16[128,1536]{1,0:T(8,128)(2,1)}, bf16[128,1536]{1,0:T(8,128)(2,1)}, u32[]{:S(2)}, u32[]{:S(2)}) collective-permute-start(bf16[128,1536]{1,0:T(8,128)(2,1)} %get-tuple-element.59), channel_id=1, source_target_pairs={{0,16},{8,24},{1,17},{9,25},{2,18},{10,26},{3,19},{11,27},{4,20},{... | collective-permute-start | bytes 1179656 | tf_op jit(solution)/shard_map/jvp()/ppermute | solution.py:54
  109.4 16.8 %collective-permute-start.1 = (bf16[128,1536]{1,0:T(8,128)(2,1)}, bf16[128,1536]{1,0:T(8,128)(2,1)}, u32[]{:S(2)}, u32[]{:S(2)}) collective-permute-start(bf16[128,1536]{1,0:T(8,128)(2,1)} %get-tuple-element.59), channel_id=1, source_target_pairs={{0,8},{8,16},{16,24},{1,9},{9,17},{17,25},{2,10},{10,18},{18,26},{... | collective-permute-start | bytes 1179656 | tf_op jit(solution)/shard_map/jvp()/ppermute | solution.py:54
  167.3 139.7 %reduce-scatter.4.cloned.1.call-start = ((), (), s32[]{:S(2)}) async-start(), calls=%async_computation.6 | async-start | bytes 2654208 | tf_op jit(solution)/shard_map/reduce_scatter | solution.py:142
  176.9 33.2 %collective-permute-start.10 = (f32[24]{0:T(128)}, f32[24]{0:T(128)}, u32[]{:S(2)}, u32[]{:S(2)}) collective-permute-start(f32[24]{0:T(128)} %fusion.66), channel_id=1, source_target_pairs={{16,0},{24,8},{17,1},{25,9},{18,2},{26,10},{19,3},{27,11},{20,4},{... | collective-permute-start | bytes 296 | tf_op jit(solution)/shard_map/transpose(jvp())/ppermute | solution.py:54
  178.2 33.1 %collective-permute-start.8 = (bf16[128,1536]{1,0:T(8,128)(2,1)}, bf16[128,1536]{1,0:T(8,128)(2,1)}, u32[]{:S(2)}, u32[]{:S(2)}) collective-permute-start(bf16[128,1536]{1,0:T(8,128)(2,1)} %get-tuple-element.81), channel_id=1, source_target_pairs={{8,0},{16,8},{24,16},{9,1},{17,9},{25,17},{10,2},{18,10},{26,18},{... | collective-permute-start | bytes 1179656 | tf_op jit(solution)/shard_map/transpose(jvp())/ppermute | solution.py:54
  179.5 31.8 %collective-permute-start.7 = (bf16[128,1536]{1,0:T(8,128)(2,1)}, bf16[128,1536]{1,0:T(8,128)(2,1)}, u32[]{:S(2)}, u32[]{:S(2)}) collective-permute-start(bf16[128,1536]{1,0:T(8,128)(2,1)} %get-tuple-element.82), channel_id=1, source_target_pairs={{16,0},{24,8},{17,1},{25,9},{18,2},{26,10},{19,3},{27,11},{20,4},{... | collective-permute-start | bytes 1179656 | tf_op jit(solution)/shard_map/transpose(jvp())/ppermute | solution.py:54
  180.8 30.5 %collective-permute-start.6 = (bf16[128,1536]{1,0:T(8,128)(2,1)}, bf16[128,1536]{1,0:T(8,128)(2,1)}, u32[]{:S(2)}, u32[]{:S(2)}) collective-permute-start(bf16[128,1536]{1,0:T(8,128)(2,1)} %get-tuple-element.83), channel_id=1, source_target_pairs={{24,0},{25,1},{26,2},{27,3},{28,4},{29,5},{30,6},{31,7}} | collective-permute-start | bytes 1179656 | tf_op jit(solution)/shard_map/transpose(jvp())/ppermute | solution.py:54
  203.7 6.4 %collective-permute-start.11 = (f32[24]{0:T(128)}, f32[24]{0:T(128)}, u32[]{:S(2)}, u32[]{:S(2)}) collective-permute-start(f32[24]{0:T(128)} %fusion.68), channel_id=1, source_target_pairs={{8,0},{16,8},{24,16},{9,1},{17,9},{25,17},{10,2},{18,10},{26,18},{... | collective-permute-start | bytes 296 | tf_op jit(solution)/shard_map/transpose(jvp())/ppermute | solution.py:54
  209.7 109.3 %reduce-scatter.6.cloned.1.call-start = ((), (), s32[]{:S(2)}) async-start(), calls=%async_computation.7 | async-start | bytes 3317760 | tf_op jit(solution)/shard_map/reduce_scatter | solution.py:142
  257.0 14.3 %collective-permute-start.9 = (bf16[3,1792]{0,1:T(8,128)(2,1)S(1)}, bf16[3,1792]{0,1:T(8,128)(2,1)S(1)}, u32[]{:S(2)}, u32[]{:S(2)}) collective-permute-start(bf16[3,1792]{0,1:T(8,128)(2,1)S(1)} %split.15), channel_id=1, source_target_pairs={{8,0},{16,8},{24,16},{9,1},{17,9},{25,17},{10,2},{18,10},{26,18},{... | collective-permute-start | bytes 32264 | tf_op jit(solution)/shard_map/transpose(jvp())/ppermute | solution.py:54
  277.1 97.0 %all-reduce.24.cloned.1.call-start = ((), (), s32[]{:S(2)}) async-start(), calls=%async_computation.9 | async-start | bytes 1916928 | tf_op jit(solution)/shard_map/psum | solution.py:143
  289.1 1.2 collective-permute-start.12
  290.3 5.6 %collective-permute-start.13 = (f32[11336]{0:T(1024)S(1)}, f32[11336]{0:T(1024)S(1)}, u32[]{:S(2)}, u32[]{:S(2)}) collective-permute-start(f32[11336]{0:T(1024)S(1)} %add.210), channel_id=1, source_target_pairs={{0,2},{1,3},{2,0},{3,1},{4,6},{5,7},{6,4},{7,5},{8,10},{9,11},{10,... | collective-permute-start | bytes 136040 | tf_op jit(solution)/shard_map/ppermute | solution.py:151
  295.9 7.7 %collective-permute-start.14 = (f32[11336]{0:T(1024)S(1)}, f32[11336]{0:T(1024)S(1)}, u32[]{:S(2)}, u32[]{:S(2)}) collective-permute-start(f32[11336]{0:T(1024)S(1)} %add.211), channel_id=1, source_target_pairs={{0,4},{1,5},{2,6},{3,7},{4,0},{5,1},{6,2},{7,3},{8,12},{9,13},{10,... | collective-permute-start | bytes 136040 | tf_op jit(solution)/shard_map/ppermute | solution.py:151
  303.6 20.7 %collective-permute-start.15 = (f32[11336]{0:T(1024)S(1)}, f32[11336]{0:T(1024)S(1)}, u32[]{:S(2)}, u32[]{:S(2)}) collective-permute-start(f32[11336]{0:T(1024)S(1)} %add.212), channel_id=1, source_target_pairs={{0,8},{8,0},{16,24},{24,16},{1,9},{9,1},{17,25},{25,17},{2,10},{10... | collective-permute-start | bytes 136040 | tf_op jit(solution)/shard_map/ppermute | solution.py:151
  324.3 4.2 %collective-permute-start.16 = (f32[11336]{0:T(1024)S(1)}, f32[11336]{0:T(1024)S(1)}, u32[]{:S(2)}, u32[]{:S(2)}) collective-permute-start(f32[11336]{0:T(1024)S(1)} %add.213), channel_id=1, source_target_pairs={{0,16},{8,24},{16,0},{24,8},{1,17},{9,25},{17,1},{25,9},{2,18},{10... | collective-permute-start | bytes 136040 | tf_op jit(solution)/shard_map/ppermute | solution.py:151
  (104 other events, 1141.0 us)
Sparse Core Ops, SparseCore 0:
  10.3 39.3 all-gather.3
  51.3 30.4 all-gather.5
  83.5 30.7 all-gather.7
  167.4 33.3 reduce-scatter.7
  209.8 40.7 reduce-scatter.3
  277.2 41.7 reduce-scatter.5
  322.8 51.1 all-reduce.23
